TPU v7x, 128 devices: a whole 4x4x4 slice. The times are simulated.
128 devices in a mesh: section: 2 (over core), dp: 64 (over z, y, x).
Axes of the slice: x: 4, y: 4, z: 4, core: 2. Of those that a mesh axis runs over, the one named last changes fastest.
Arguments:
- inputs: bfloat16 [128, 128, 4096], P('dp'), may hold values from -6 to 6
- upstream: bfloat16 [128, 128, 4096], P('dp'), may hold values from -6 to 6
- doc_blocks: int32 [128, 2], P('dp'), may hold values from 0 to 1, as said below
- gain: bfloat16 [2, 4096], P('section', 'dp'), may hold values from 0.5 to 1.5
- key_weight: bfloat16 [2, 4096, 512], P('section', 'dp'), may hold values from -0.09375 to 0.09375
- value_weight: bfloat16 [2, 4096, 512], P('section', 'dp'), may hold values from -0.09375 to 0.09375
Outputs:
- grad_inputs: bfloat16 [2, 128, 128, 4096], P('section', 'dp')
- grad_key: float32 [2, 4096, 512], P('section', 'dp')
- grad_value: float32 [2, 4096, 512], P('section', 'dp')
- grad_gain: float32 [2, 4096], P('section', 'dp')
Inputs may be any that keep to these rules, and one draw needn't show every extreme that they name: `doc_blocks`: each row starts with document 0, and the number rises by 0 or 1 from one block to the next.
All inputs are finite; a program needn't handle non-finite values.
Results may differ from a plain program's by a relative error of at most 0.02.
Values may be sent and summed in bfloat16 or wider, within the bound.
A program may use at most 192 MiB of HBM per device.

v0:
```python
from functools import partial

import jax
import jax.numpy as jnp
from jax import lax
from jax.sharding import PartitionSpec as P

HEAD_DIM = 128
KV_HEADS = 4
BLOCK = 64


def from_behind(x, axis, by):
    peers = lax.axis_size(axis)
    pairs = [(i, i + by) for i in range(peers) if 0 <= i + by < peers]
    return lax.ppermute(x, axis, pairs)


def normed(activations, gain_values):
    widened = activations.astype(jnp.float32)
    factor = lax.rsqrt(jnp.mean(widened * widened, axis=-1, keepdims=True) + 1e-05)
    return (widened * factor * gain_values).astype(jnp.bfloat16)


def project(hidden, key_weight, value_weight):
    batch_rows, length, model_width = hidden.shape
    flat_rows = hidden.reshape(batch_rows * length, model_width)
    key_rows = jnp.dot(flat_rows, key_weight, preferred_element_type=jnp.float32).astype(
        jnp.bfloat16
    )
    value_rows = jnp.dot(flat_rows, value_weight, preferred_element_type=jnp.float32).astype(
        jnp.bfloat16
    )
    return (key_rows.reshape(batch_rows, length, -1), value_rows.reshape(batch_rows, length, -1))


def attend(hidden, key_rows, value_rows, documents):
    batch_rows, length, model_width = hidden.shape
    groups = model_width // HEAD_DIM // KV_HEADS
    queries = hidden.reshape(batch_rows, length, KV_HEADS, groups, HEAD_DIM)
    key_heads = key_rows.reshape(batch_rows, length, KV_HEADS, HEAD_DIM)
    value_heads = value_rows.reshape(batch_rows, length, KV_HEADS, HEAD_DIM)
    score_scale = HEAD_DIM ** (-0.5)
    key_docs = jnp.repeat(documents, BLOCK, axis=1)
    pieces = []
    for block_index in range(length // BLOCK):
        query_block = queries[:, block_index * BLOCK : (block_index + 1) * BLOCK]
        scores = (
            jnp.einsum(
                "bqhgd,bkhd->bhgqk", query_block, key_heads, preferred_element_type=jnp.float32
            )
            * score_scale
        )
        same_doc = key_docs == documents[:, block_index : block_index + 1]
        query_pos = block_index * BLOCK + jnp.arange(BLOCK)
        causal = jnp.arange(length)[None, :] <= query_pos[:, None]
        allowed = same_doc[:, None, None, None, :] & causal[None, None, None, :, :]
        scores = jnp.where(allowed, scores, -1e30)
        weights = jnp.exp(scores)
        probability = (weights / jnp.sum(weights, axis=-1, keepdims=True)).astype(jnp.bfloat16)
        mixture = jnp.einsum(
            "bhgqk,bkhd->bqhgd", probability, value_heads, preferred_element_type=jnp.float32
        )
        pieces.append(mixture.reshape(batch_rows, BLOCK, model_width))
    return jnp.concatenate(pieces, axis=1)


def layer_forward(activations, gain_values, key_weight, value_weight, documents):
    hidden = normed(activations, gain_values)
    key_rows, value_rows = project(hidden, key_weight, value_weight)
    return (
        activations.astype(jnp.float32) + attend(hidden, key_rows, value_rows, documents)
    ).astype(jnp.bfloat16)


def layer_backward(activations, cotangent, gain_values, key_weight, value_weight, documents):
    hidden, norm_back = jax.vjp(normed, activations, gain_values)
    key_rows, value_rows = project(hidden, key_weight, value_weight)
    core_out, core_back = jax.vjp(
        partial(attend, documents=documents), hidden, key_rows, value_rows
    )
    query_grad, key_grad, value_grad = core_back(cotangent.astype(jnp.float32))
    key_flat = key_grad.reshape(-1, key_weight.shape[1])
    value_flat = value_grad.reshape(-1, value_weight.shape[1])
    through = jnp.dot(key_flat, key_weight.T, preferred_element_type=jnp.float32) + jnp.dot(
        value_flat, value_weight.T, preferred_element_type=jnp.float32
    )
    hidden_grad = (query_grad.astype(jnp.float32) + through.reshape(hidden.shape)).astype(
        jnp.bfloat16
    )
    input_grad, gain_grad = norm_back(hidden_grad)
    total = (cotangent.astype(jnp.float32) + input_grad.astype(jnp.float32)).astype(jnp.bfloat16)
    return (total, gain_grad, hidden, key_grad, value_grad)


def shards(inputs, upstream, doc_blocks, gain, key_weight, value_weight):
    section_count = lax.axis_size("section")
    section_index = lax.axis_index("section")
    gain_whole, key_whole, value_whole = (
        lax.all_gather(gain[0], "dp", axis=0, tiled=True),
        lax.all_gather(key_weight[0], "dp", axis=0, tiled=True),
        lax.all_gather(value_weight[0], "dp", axis=0, tiled=True),
    )
    gain_values = gain_whole.astype(jnp.float32)
    micro_count, seq_length, model_width = inputs.shape
    key_width = key_whole.shape[1]
    rounds = micro_count // micro_count
    steps = section_count + rounds - 1
    empty_rows = jnp.zeros((micro_count, seq_length, model_width), jnp.bfloat16)

    def forward_step(carry, step_index):
        inbox, saved = carry
        slot_index = step_index - section_index
        active = (slot_index >= 0) & (slot_index < rounds)
        entering = jnp.where(section_index == 0, inputs, inbox)
        result = lax.cond(
            active,
            lambda: layer_forward(entering, gain_values, key_whole, value_whole, doc_blocks),
            lambda: empty_rows,
        )
        saved = jnp.where(active, entering, saved)
        inbox = from_behind(result, "section", 1)
        return ((inbox, saved), None)

    (unused_box, saved), unused_out = lax.scan(
        forward_step, (empty_rows, jnp.zeros_like(inputs)), jnp.arange(steps)
    )
    start_totals = (
        jnp.zeros((model_width, key_width), jnp.float32),
        jnp.zeros((model_width, key_width), jnp.float32),
        jnp.zeros((model_width,), jnp.float32),
    )

    def backward_step(carry, step_index):
        inbox, grad_rows, totals = carry
        slot_index = step_index - (section_count - 1 - section_index)
        active = (slot_index >= 0) & (slot_index < rounds)
        cotangent = jnp.where(section_index == section_count - 1, upstream, inbox)
        entering = saved

        def working():
            flowing, gain_grad, hidden, key_grad, value_grad = layer_backward(
                entering, cotangent, gain_values, key_whole, value_whole, doc_blocks
            )
            hidden_flat = hidden.reshape(-1, model_width)
            key_part = jnp.einsum(
                "td,tk->dk",
                hidden_flat,
                key_grad.reshape(-1, key_width),
                preferred_element_type=jnp.float32,
            )
            value_part = jnp.einsum(
                "td,tk->dk",
                hidden_flat,
                value_grad.reshape(-1, key_width),
                preferred_element_type=jnp.float32,
            )
            return (flowing, gain_grad, key_part, value_part)

        def resting():
            return (
                empty_rows,
                jnp.zeros((model_width,), jnp.float32),
                jnp.zeros((model_width, key_width), jnp.float32),
                jnp.zeros((model_width, key_width), jnp.float32),
            )

        flowing, gain_grad, key_part, value_part = lax.cond(active, working, resting)
        totals = (totals[0] + key_part, totals[1] + value_part, totals[2] + gain_grad)
        grad_rows = jnp.where(active, flowing, grad_rows)
        inbox = from_behind(flowing, "section", -1)
        return ((inbox, grad_rows, totals), None)

    (unused_box, grad_rows, totals), unused_out = lax.scan(
        backward_step, (empty_rows, jnp.zeros_like(inputs), start_totals), jnp.arange(steps)
    )
    key_share, value_share, gain_share = (
        lax.psum_scatter(totals[0], "dp", scatter_dimension=0, tiled=True),
        lax.psum_scatter(totals[1], "dp", scatter_dimension=0, tiled=True),
        lax.psum_scatter(totals[2], "dp", scatter_dimension=0, tiled=True),
    )
    return (grad_rows[None], key_share[None], value_share[None], gain_share[None])


def solution(mesh):
    in_specs = (
        P("dp", None, None),
        P("dp", None, None),
        P("dp", None),
        P("section", "dp"),
        P("section", "dp", None),
        P("section", "dp", None),
    )
    out_specs = (
        P("section", "dp", None, None),
        P("section", "dp", None),
        P("section", "dp", None),
        P("section", "dp"),
    )
    return jax.shard_map(shards, mesh=mesh, in_specs=in_specs, out_specs=out_specs, check_vma=False)
```

profile of v0, /device:TPU:0, one launch (start us, length us, event | category | flops | bytes accessed | tf_op | source)
XLA Modules:
  0.0 1249.8 jit_solution(5299405214661399577)
XLA Ops:
  11.7 183.4 %all-reduce.2 = bf16[4096]{0:T(1024)(128)(2,1)S(1)} all-reduce(bf16[4096]{0:T(1024)(128)(2,1)S(1)} %dynamic-update-slice), channel_id=2, replica_groups=mesh['section'=2,'dp'=64] {'dp'}, use_global_device_ids=true, to_apply=%add.2 | all-reduce | flops 4096 | bytes 16384
  197.5 104.5 %while.35 = (s32[]{:T(128)}, bf16[2,128,4096]{2,1,0:T(8,128)(2,1)}, bf16[2,128,4096]{2,1,0:T(8,128)(2,1)S(1)}, s32[2]{0:T(128)S(1)}, s32[]{:T(128)}, /*index=5*/...) while((s32[]{:T(128)}, bf16[2,128,4096]{2,1,0:T(8,128)(2,1)}, ...), condition=%wide.region_6.7_spmd.clone, body=%wide.region_0.6_spmd.clone.sunk | while | flops 2706678528 | bytes 128673760 | solution.py:125
  202.9 41.0 %conditional.6 = (bf16[2,128,4096]{2,1,0:T(8,128)(2,1)}) conditional(s32[]{:T(128)} %convert_element_type.276, () %tuple.106, (bf16[2,128,4096]{2,1,0:T(8,128)(2,1)}, f32[4096]{0:T(1024)S(1)}, bf16[4096,512]{1,0:T(8,128)(2,1)}, s32[2,2]{0,1:T(2,128)S(1)}, bf16[4096,512]{1,0:T(8,128)(2,1)}) %tuple.107), branch_computations={%region_1.1_spmd, %region_2.5_spmd} | conditional | flops 2703532800 | bytes 109799128 | solution.py:116
  209.8 4.1 copy.92
  239.0 4.8 fusion.3
  256.2 43.0 %collective-permute-start = (bf16[2,128,4096]{2,1,0:T(8,128)(2,1)}, bf16[2,128,4096]{2,1,0:T(8,128)(2,1)}, u32[]{:S(2)}, u32[]{:S(2)}) collective-permute-start(bf16[2,128,4096]{2,1,0:T(8,128)(2,1)} %get-tuple-element.872), channel_id=1, source_target_pairs={{0,64},{1,65},{2,66},{3,67},{4,68},{5,69},{6,70},{7,71},{8,72},{9,... | collective-permute-start | bytes 6291464 | tf_op jit(solution)/shard_map/while/body/eval_jaxpr/ppermute | solution.py:16
  303.5 210.9 %while.36 = (s32[]{:T(128)}, bf16[2,128,4096]{2,1,0:T(8,128)(2,1)}, bf16[2,128,4096]{2,1,0:T(8,128)(2,1)}, f32[4096,512]{1,0:T(8,128)}, f32[4096,512]{1,0:T(8,12...) while((s32[]{:T(128)}, bf16[2,128,4096]{2,1,0:T(8,128)(2,1)}, ...), condition=%wide.region_17.18_spmd.clone, body=%wide.region_7.17_spmd.clone.sunk | while | flops 7855782400 | bytes 426075072 | solution.py:174
  325.1 10.9 conditional.7
  325.1 4.3 broadcast.227
  329.5 4.3 broadcast.227.clone
  339.6 11.5 select_add_fusion.5
  351.1 57.5 %collective-permute-done.1 = bf16[2,128,4096]{2,1,0:T(8,128)(2,1)} collective-permute-done((bf16[2,128,4096]{2,1,0:T(8,128)(2,1)}, bf16[2,128,4096]{2,1,0:T(8,128)(2,1)}, u32[]{:S(2)}, u32[]{:S(2)}) %collective-permute-start.1) | collective-permute-done | bytes 2097184 | tf_op jit(solution)/shard_map/while/body/eval_jaxpr/ppermute | solution.py:16
  409.8 79.9 %conditional.7 = (bf16[2,128,4096]{2,1,0:T(8,128)(2,1)}, f32[4096]{0:T(1024)}, f32[4096,512]{1,0:T(8,128)}, f32[4096,512]{1,0:T(8,128)}) conditional(s32[]{:T(128)} %convert_element_type.277, () %tuple.110, (pred[]{:T(512)}, bf16[2,128,4096]{2,1,0:T(8,128)(2,1)}, bf16[2,128,4096]{2,1,0:T(8,128)(2,1)}, s32[2,2]{0,1:T(2,128)S(1)}, ...), branch_computations={%region_8.8_spmd, %region_9.16_spmd} | conditional | flops 7845288448 | bytes 360882464 | solution.py:168
  415.6 4.1 copy.104
  419.6 4.0 fusion.75
  433.4 4.5 fusion.103
  464.9 5.3 copy.115
  470.3 5.6 copy.118
  475.9 6.2 fusion.29
  485.1 4.6 fusion.106
  495.5 18.9 %select_add_fusion.5 = (f32[4096,512]{1,0:T(8,128)}, f32[4096,512]{1,0:T(8,128)}) fusion(f32[4096,512]{1,0:T(8,128)} %get-tuple-element.769, f32[4096,512]{1,0:T(8,128)} %get-tuple-element.842, pred[]{:T(512)S(6)} %compare.9, f32[4096,512]{1,0:T(8,128)} %get-tuple-element.770, f32[4096,512]{1,0:T(8,128)} %get-tuple-element.841), kind=kLoop, calls=%fused_computation.175.clone.1 | loop fusion | flops 8388608 | bytes 50331648 | tf_op jit(solution)/shard_map/while/body/eval_jaxpr/add | solution.py:169
  515.7 341.8 %all-reduce.3 = f32[4096]{0:T(1024)S(1)} all-reduce(f32[4096]{0:T(1024)S(1)} %copy-done.26), channel_id=7, replica_groups=mesh['section'=2,'dp'=64] {'dp'}, use_global_device_ids=true, to_apply=%region_20.21.clone | all-reduce | flops 4096 | bytes 32768
  858.0 19.9 %reduce-scatter.3.cloned.1.call-done = f32[64,512]{1,0:T(8,128)} async-done(((f32[4096,512]{1,0:T(8,128)}), f32[64,512]{1,0:T(8,128)}) %reduce-scatter.3.cloned.1.call-update) | async-done | bytes 131088 | tf_op jit(solution)/shard_map/reduce_scatter | solution.py:178
  877.9 365.0 %reduce-scatter.5.cloned.1.call-done = f32[64,512]{1,0:T(8,128)} async-done(((f32[4096,512]{1,0:T(8,128)}), f32[64,512]{1,0:T(8,128)}) %reduce-scatter.5.cloned.1.call-update) | async-done | bytes 131088 | tf_op jit(solution)/shard_map/reduce_scatter | solution.py:179
  (212 shorter events, 119.3 us)
Async XLA Ops:
  7.2 188.8 %all-gather.6.cloned.1.call-start = ((), (), s32[]{:S(2)}) async-start(), calls=%async_computation.4 | async-start | bytes 4259840 | tf_op jit(solution)/shard_map/all_gather | solution.py:102
  7.9 188.1 %all-gather.8.cloned.1.call-start = ((), (), s32[]{:S(2)}) async-start(), calls=%async_computation.5 | async-start | bytes 4259840 | tf_op jit(solution)/shard_map/all_gather | solution.py:101
  8.6 869.3 %reduce-scatter.3.cloned.1.call-start = ((), (), s32[]{:S(2)}) async-start(), calls=%async_computation.2 | async-start | bytes 8519680 | tf_op jit(solution)/shard_map/reduce_scatter | solution.py:178
  213.9 3.9 copy-start.7
  243.9 5.4 collective-permute-start
  256.2 45.7 %collective-permute-start = (bf16[2,128,4096]{2,1,0:T(8,128)(2,1)}, bf16[2,128,4096]{2,1,0:T(8,128)(2,1)}, u32[]{:S(2)}, u32[]{:S(2)}) collective-permute-start(bf16[2,128,4096]{2,1,0:T(8,128)(2,1)} %get-tuple-element.872), channel_id=1, source_target_pairs={{0,64},{1,65},{2,66},{3,67},{4,68},{5,69},{6,70},{7,71},{8,72},{9,... | collective-permute-start | bytes 6291464 | tf_op jit(solution)/shard_map/while/body/eval_jaxpr/ppermute | solution.py:16
  336.0 72.5 %collective-permute-start.1 = (bf16[2,128,4096]{2,1,0:T(8,128)(2,1)}, bf16[2,128,4096]{2,1,0:T(8,128)(2,1)}, u32[]{:S(2)}, u32[]{:S(2)}) collective-permute-start(bf16[2,128,4096]{2,1,0:T(8,128)(2,1)} %get-tuple-element.768), channel_id=1, source_target_pairs={{64,0},{65,1},{66,2},{67,3},{68,4},{69,5},{70,6},{71,7},{72,8},{73... | collective-permute-start | bytes 6291464 | tf_op jit(solution)/shard_map/while/body/eval_jaxpr/ppermute | solution.py:16
  339.6 11.5 copy-start.25
  339.6 69.0 %copy-start.28 = (s32[2,2]{0,1:T(2,128)S(1)}, s32[2,2]{0,1:T(2,128)}, u32[]{:S(2)}) copy-start(s32[2,2]{0,1:T(2,128)} %copy-done.27) | copy-start | bytes 52 | tf_op jit(solution)/shard_map/while
  339.6 69.0 %copy-start.40 = (s32[2]{0:T(128)S(1)}, s32[2]{0:T(128)}, u32[]{:S(2)}) copy-start(s32[2]{0:T(128)} %copy-done.39) | copy-start | bytes 28 | tf_op jit(solution)/shard_map/while
  414.9 4.7 copy-start.33
  414.9 4.7 copy-start.35
  419.6 4.1 copy-start.21
  423.7 4.2 copy-start.10
  433.3 4.7 copy-start.18
  433.4 4.5 copy-start.12
  470.3 5.7 copy-start.30
  475.9 6.2 copy-start.32
  475.9 6.2 copy-start.5
  489.7 24.8 %collective-permute-start.1 = (bf16[2,128,4096]{2,1,0:T(8,128)(2,1)}, bf16[2,128,4096]{2,1,0:T(8,128)(2,1)}, u32[]{:S(2)}, u32[]{:S(2)}) collective-permute-start(bf16[2,128,4096]{2,1,0:T(8,128)(2,1)} %get-tuple-element.768), channel_id=1, source_target_pairs={{64,0},{65,1},{66,2},{67,3},{68,4},{69,5},{70,6},{71,7},{72,8},{73... | collective-permute-start | bytes 6291464 | tf_op jit(solution)/shard_map/while/body/eval_jaxpr/ppermute | solution.py:16
  495.5 18.9 %copy-start.25 = (f32[4096]{0:T(1024)}, f32[4096]{0:T(1024)S(1)}, u32[]{:S(2)}) copy-start(f32[4096]{0:T(1024)S(1)} %select_add_fusion.6) | copy-start | bytes 49156 | tf_op jit(solution)/shard_map/while
  495.5 19.0 %copy-start.28 = (s32[2,2]{0,1:T(2,128)S(1)}, s32[2,2]{0,1:T(2,128)}, u32[]{:S(2)}) copy-start(s32[2,2]{0,1:T(2,128)} %copy-done.27) | copy-start | bytes 52 | tf_op jit(solution)/shard_map/while
  495.5 19.0 %copy-start.40 = (s32[2]{0:T(128)S(1)}, s32[2]{0:T(128)}, u32[]{:S(2)}) copy-start(s32[2]{0:T(128)} %copy-done.39) | copy-start | bytes 28 | tf_op jit(solution)/shard_map/while
  514.5 728.4 %reduce-scatter.5.cloned.1.call-start = ((), (), s32[]{:S(2)}) async-start(), calls=%async_computation.3 | async-start | bytes 8519680 | tf_op jit(solution)/shard_map/reduce_scatter | solution.py:179
  (31 other events, 53.9 us)
Sparse Core Ops, SparseCore 0:
  10.9 71.5 all-gather.5
  85.4 66.3 all-gather.7
  514.6 363.2 reduce-scatter.2
  880.8 362.1 reduce-scatter.4
where the time goes:
time: 1260 us; the launch traced here: 1250 us
  blocking collectives  525 us (42%)
  waiting for transfers between devices  450 us (36%)
  other arithmetic  73.7 us (6%)
  local copies, waits for them, and re-layouts  67.8 us (5%)
  starting transfers between devices  48.3 us (4%)
  matrix products  45.7 us (4%)
  loops' own time  23.8 us (2%)
  between operations  15.6 us (1%)
    unnamed x2, blocking collectives  525 us
    reduce_scatter x1, waiting for transfers between devices, shards(): lax.psum_scatter(totals[1], 'dp', scatter_dimension=0, tiled=True)  365 us
    ppermute x4, waiting for transfers between devices, from_behind(): return lax.ppermute(x, axis, pairs)  63 us
    ppermute x4, starting transfers between devices, from_behind(): return lax.ppermute(x, axis, pairs)  48.1 us
    add x2, other arithmetic, backward_step(): totals[1] + value_part  30.4 us
  transfers between devices with their start and end apart: 8, of which 5 were waited for; matrix products, arithmetic and copies ran while one was open for 3% of the time, Pallas kernels for 0%

commit v1 on v0

v1 whole, which is shorter than its diff:
```python
import jax
import jax.numpy as jnp
from jax import lax
from jax.experimental import pallas as pl
from jax.experimental.pallas import tpu as pltpu
from jax.sharding import PartitionSpec as P

HEAD_DIM = 128
BLOCK = 64
ROWS = 64
STRIDE = {"x": 1, "y": 4, "z": 16}
COLOURS = ((("x", "y", "z"), 0, 384), (("z", "y", "x"), 384, 384), (("x", "z", "y"), 768, 256))
OWN, AFTER, FAR, BEFORE = 0, 1, 2, 3
MESH = pl.DeviceIdType.MESH


class Torus:
    def __init__(self):
        self.section = lax.axis_index("section")
        self.me = lax.axis_index("dp")
        self.pos = {"x": lax.rem(self.me, 4), "y": lax.rem(self.me // 4, 4), "z": self.me // 16}

    def at(self, axis, delta):
        return lax.rem(self.pos[axis] + delta, 4)

    def peer(self, axis, delta):
        return (self.section, self.me + (self.at(axis, delta) - self.pos[axis]) * STRIDE[axis])

    def other(self):
        return (1 - self.section, self.me)

    def barrier(self):
        sem = pltpu.get_barrier_semaphore()
        for axis in "xyz":
            for delta in (1, 2, 3):
                pl.semaphore_signal(sem, inc=1, device_id=self.peer(axis, delta), device_id_type=MESH)
        pl.semaphore_signal(sem, inc=1, device_id=self.other(), device_id_type=MESH)
        pl.semaphore_wait(sem, 10)


def remote(src, dst, sems, index, device):
    return pltpu.make_async_remote_copy(
        src_ref=src, dst_ref=dst, send_sem=sems[0].at[index], recv_sem=sems[1].at[index],
        device_id=device, device_id_type=MESH)


def half(ref, which):
    size = ref.shape[0] // 2
    return ref.at[pl.ds(which * size, size)]


def add_into(dst, *others):
    for i in range(dst.shape[0]) if len(dst.shape) > 2 else (Ellipsis,):
        total = dst[i].astype(jnp.float32)
        for other in others:
            total = total + other[i].astype(jnp.float32)
        dst[i] = total.astype(dst.dtype)


class Ring:
    def __init__(self, torus, axis, sems, index, sends):
        self.torus, self.axis, self.sems, self.index, self.sends = torus, axis, sems, index, sends

    def send(self, k, src, dst, delta):
        copy = remote(src, dst, self.sems, self.index + (k,), self.torus.peer(self.axis, delta))
        copy.start()
        self.sends.append(copy)

    def arrived(self, k, ref):
        remote(ref, ref, self.sems, self.index + (k,), self.torus.peer(self.axis, 1)).wait_recv()


class Gather(Ring):
    def __init__(self, torus, axis, sems, index, sends, ref_at):
        super().__init__(torus, axis, sems, index, sends)
        self.blocks = [ref_at(torus.at(axis, d)) for d in range(4)]

    def start(self):
        own = self.blocks[OWN]
        for k, which, delta in ((0, 0, 1), (2, 1, 3), (1, 1, 1), (3, 0, 3)):
            self.send(k, half(own, which), half(own, which), delta)

    def forward(self):
        for k, block, which, delta in ((0, BEFORE, 0, 1), (2, AFTER, 1, 3)):
            ref = half(self.blocks[block], which)
            self.arrived(k, ref)
            self.send(4 + k // 2, ref, ref, delta)

    def near(self):
        self.arrived(1, half(self.blocks[BEFORE], 1))
        self.arrived(3, half(self.blocks[AFTER], 0))

    def finish(self):
        self.arrived(4, half(self.blocks[FAR], 0))
        self.arrived(5, half(self.blocks[FAR], 1))


class Scatter(Ring):
    def __init__(self, torus, axis, sems, index, sends, ref_at, inbox):
        super().__init__(torus, axis, sems, index, sends)
        self.blocks = [ref_at(torus.at(axis, d)) for d in range(4)]
        self.inbox = inbox

    def out(self, k, block, which, delta):
        self.send(k, half(self.blocks[block], which), self.inbox.at[k], delta)

    def into(self, block, which, *slots):
        for k in slots:
            self.arrived(k, self.inbox.at[k])
        add_into(half(self.blocks[block], which), *[self.inbox.at[k] for k in slots])

    def start_far(self):
        self.out(0, FAR, 0, 1)
        self.out(1, FAR, 1, 3)

    def start_after(self):
        self.out(2, AFTER, 1, 1)

    def start_before(self):
        self.out(3, BEFORE, 0, 3)

    def start(self):
        self.start_far()
        self.start_after()
        self.start_before()

    def forward(self):
        self.into(AFTER, 0, 0)
        self.out(4, AFTER, 0, 1)
        self.into(BEFORE, 1, 1)
        self.out(5, BEFORE, 1, 3)

    def finish(self):
        self.into(OWN, 0, 3, 4)
        self.into(OWN, 1, 2, 5)


class Direct:
    def __init__(self, torus, axis, sems, index, sends, ref_at, inbox=None):
        self.ring = Ring(torus, axis, sems, index, sends)
        self.blocks = [ref_at(torus.at(axis, d)) for d in range(4)]
        self.inbox = inbox

    def start(self):
        for k, delta in ((0, 2), (1, 1), (2, 3)):
            if self.inbox is None:
                self.ring.send(k, self.blocks[OWN], self.blocks[OWN], delta)
            else:
                self.ring.send(k, self.blocks[delta], self.inbox.at[k], delta)

    def finish(self):
        for k, delta in ((0, 2), (1, 1), (2, 3)):
            self.ring.arrived(k, self.blocks[4 - delta] if self.inbox is None else self.inbox.at[k])
        if self.inbox is not None:
            add_into(self.blocks[OWN], *[self.inbox.at[k] for k in range(3)])


def chunk_of(bufs, c, z, y):
    index = {"z": z, "y": y, "x": slice(None)}
    first, mid, last = COLOURS[c][0]
    return bufs[c].at[index[last], index[mid], index[first]]


def dot(a, b):
    return jnp.dot(a, b, preferred_element_type=jnp.float32)


def dot_nt(a, b):
    return lax.dot_general(a, b, (((1,), (1,)), ((), ())), preferred_element_type=jnp.float32)


def rows(i, size):
    return pl.ds(pl.multiple_of(i * size, size), size)


def layer_kernel(
    docs_ref, gain_ref, key_ref, value_ref, inputs_ref, upstream_ref,
    out_ref, key_out, value_out, gain_out,
    g0, g1, g2, gg, b0, b1, b2, bg, r20, r21, r22, r10, r11, r12, r00, r01, r02, q2, q1, q0,
    nat, x_t, out_t, m_t, m_nat, c_t, dh_t, p_t, kv, kv_t, dkv, dkv_r, dkv_t, gcol, ggcol, bias, stat,
    local_sem, send_sem, recv_sem, gsend_sem, grecv_sem, ssend_sem, srecv_sem, sgsend_sem, sgrecv_sem, cross_send, cross_recv,
    go_sem,
):
    torus = Torus()
    section, pos = torus.section, torus.pos
    bufs, sums = (g0, g1, g2), (b0, b1, b2)
    first_core, second_core = section == 0, section == 1
    odd = lax.rem(torus.me, 2) == 1
    colours = range(3)
    axes_of = [axes for axes, _, _ in COLOURS]

    def own_place(bufs, c):
        first, mid, last = axes_of[c]
        return bufs[c].at[pos[last], pos[mid], pos[first]]

    local = [
        pltpu.make_async_copy(key_ref.at[:, pl.ds(0, 384)], own_place(bufs, 0), local_sem.at[0]),
        pltpu.make_async_copy(key_ref.at[:, pl.ds(384, 128)], own_place(bufs, 1).at[:, pl.ds(0, 128)], local_sem.at[1]),
        pltpu.make_async_copy(value_ref.at[:, pl.ds(0, 256)], own_place(bufs, 1).at[:, pl.ds(128, 256)], local_sem.at[2]),
        pltpu.make_async_copy(value_ref.at[:, pl.ds(256, 256)], own_place(bufs, 2), local_sem.at[3]),
    ]
    for copy in local:
        copy.start()
    load_inputs = pltpu.make_async_copy(inputs_ref, nat, local_sem.at[5])
    load_upstream = pltpu.make_async_copy(upstream_ref, nat, local_sem.at[6])
    pl.when(first_core)(load_inputs.start)
    pl.when(second_core)(load_upstream.start)
    gain_row = gain_ref[...].astype(jnp.float32)
    still = jnp.zeros_like(gain_row)
    placed = jnp.where(odd, jnp.concatenate([still, gain_row], axis=1), jnp.concatenate([gain_row, still], axis=1))
    gg[pos["z"], pos["y"], pos["x"]] = jnp.broadcast_to(placed, (8, 128))
    torus.barrier()
    for copy in local:
        copy.wait()


    def turn(src, dst, start, count):
        def body(i, carry):
            dst[rows(start + i, 512), :] = src[:, rows(start + i, 512)].T
            return carry

        lax.fori_loop(0, count, body, 0)

    lane = lax.broadcasted_iota(jnp.int32, (128, 128), 1)

    def gain_columns():
        ggcol[...] = jnp.zeros_like(ggcol)
        for j in range(32):
            i = 2 * j
            ggcol[j:j + 1, :] = (gg[i // 16, i // 4 % 4, i % 4] + gg[i // 16, i // 4 % 4, i % 4 + 1])[0:1]
        gcol[...] = ggcol[...].T

    def gain_column(j):
        return jnp.sum(jnp.where(lane == j, gcol[...], 0.0), axis=1, keepdims=True)

    def prepare(start, count):
        def body(i, total):
            x = x_t[rows(start + i, 128), :].astype(jnp.float32)
            m = (x * gain_column(start + i)).astype(jnp.bfloat16)
            m_t[rows(start + i, 128), :] = m
            m_nat[:, rows(start + i, 128)] = m.T
            return total + jnp.sum((x * x).reshape(16, 8, 256), axis=0)

        return lax.fori_loop(0, count, body, jnp.zeros((8, 256), jnp.float32))

    def factors(total):
        mean = jnp.sum(total, axis=0, keepdims=True) * (1.0 / 4096.0)
        stat[0:8] = jnp.broadcast_to(lax.rsqrt(mean + 1e-05), (8, 256))

    def factor_column():
        return stat[0:8].T[:, 0:1]

    def project():
        for c, (_, start, w) in enumerate(COLOURS):
            def body(z, total, c=c, w=w):
                weight = jnp.concatenate([chunk_of(bufs, c, z, y)[...].reshape(256, w) for y in range(4)], axis=0)
                return total + dot(m_nat[:, rows(z, 1024)], weight)

            total = lax.fori_loop(0, 4, body, jnp.zeros((256, w), jnp.float32))
            kv[:, start:start + w] = (total * factor_column()).astype(jnp.bfloat16)
        kv_t[...] = kv[...].T

    def masks():
        key = lax.broadcasted_iota(jnp.int32, (128, 128), 0)
        query = lax.broadcasted_iota(jnp.int32, (128, 128), 1)
        same_block = (key >= BLOCK) == (query >= BLOCK)
        for b in range(2):
            together = jnp.broadcast_to(docs_ref[b, 0] == docs_ref[b, 1], (128, 128))
            allowed = (key <= query) & (same_block | together)
            bias[b] = jnp.where(allowed, 0.0, -1e30)

    scale = HEAD_DIM ** -0.5

    def heads(ref, h, b):
        return jnp.concatenate([ref[rows(h * 8 + j, 128), rows(b, 128)] for j in range(8)], axis=1)

    def token_row(row, b):
        return jnp.concatenate([stat[row:row + 1, rows(b, 128)]] * 8, axis=1)

    def probabilities(i):
        h, b = i // 2, lax.rem(i, 2)
        scores = dot(kv[rows(b, 128), rows(h, 128)], heads(m_t, h, b))
        weights = jnp.exp(scores * (token_row(0, b) * scale) + jnp.concatenate([bias[b]] * 8, axis=1))
        share = 1.0 / jnp.sum(weights, axis=0, keepdims=True)
        p_t[i] = (weights * share).astype(jnp.bfloat16)

    def attention_forward():
        def body(i, carry):
            probabilities(i)
            return carry

        lax.fori_loop(0, 8, body, 0)

    def mix(i):
        h, b = i // 2, i % 2
        mixed = dot(kv_t[512 + 128 * h:640 + 128 * h, 128 * b:128 * b + 128], p_t[i])
        for j in range(8):
            at = (pl.ds((8 * h + j) * 128, 128), pl.ds(b * 128, 128))
            out_t[at] = (x_t[at].astype(jnp.float32) + mixed[:, 128 * j:128 * j + 128]).astype(jnp.bfloat16)

    def attention_backward():
        def body(i, carry):
            h, b = i // 2, lax.rem(i, 2)
            c = heads(c_t, h, b)
            p = p_t[i]
            d_p = dot(kv[rows(b, 128), rows(4 + h, 128)], c)
            p_wide = p.astype(jnp.float32)
            inner = jnp.sum(p_wide * d_p, axis=0, keepdims=True)
            d_s = p_wide * (d_p - inner) * scale
            dkv[rows(b, 128), rows(4 + h, 128)] = dot_nt(p, c).astype(jnp.bfloat16)
            d_s_r = (d_s * token_row(0, b)).astype(jnp.bfloat16)
            dkv[rows(b, 128), rows(h, 128)] = dot_nt(d_s_r, heads(m_t, h, b)).astype(jnp.bfloat16)
            d_q = dot(kv_t[rows(h, 128), rows(b, 128)], d_s.astype(jnp.bfloat16))
            for j in range(8):
                dh_t[rows(h * 8 + j, 128), rows(b, 128)] = d_q[:, 128 * j:128 * j + 128].astype(jnp.bfloat16)
            return carry

        lax.fori_loop(0, 8, body, 0)
        dkv_t[...] = dkv[...].T
        dkv_r[...] = (dkv[...].astype(jnp.float32) * factor_column()).astype(jnp.bfloat16)

    def weight_grads(c, delta):
        axes, start, w = COLOURS[c]
        mid = torus.at(axes[1], delta)

        def body(n, carry):
            z, y = (n, mid) if axes[1] == "y" else (mid, n)
            part = dot(m_t[rows(z * 4 + y, 256), :], dkv_r[:, start:start + w]).astype(jnp.bfloat16)
            chunk_of(sums, c, z, y)[...] = part.reshape(4, ROWS, w)
            return carry

        lax.fori_loop(0, 4, body, 0)

    def through():
        ggcol[...] = jnp.zeros_like(ggcol)

        def body(i, carry):
            z, y = i // 4, lax.rem(i, 4)
            weight = jnp.concatenate(
                [chunk_of(bufs, c, z, y)[...].reshape(256, w) for c, (_, _, w) in enumerate(COLOURS)], axis=1)
            d_h = (dh_t[rows(i, 256), :].astype(jnp.float32) + dot(weight, dkv_t[...])).astype(jnp.bfloat16)
            dh_t[rows(i, 256), :] = d_h
            a = x_t[rows(i, 256), :].astype(jnp.float32)
            both = d_h.astype(jnp.float32) * a
            gains = jnp.concatenate([gain_column(2 * i), gain_column(2 * i + 1)], axis=0)
            by_gain = jnp.sum(both * stat[0:1], axis=1, keepdims=True)
            ggcol[...] = jnp.where(
                lane == 2 * i, by_gain[0:128], jnp.where(lane == 2 * i + 1, by_gain[128:256], ggcol[...]))
            return carry + jnp.sum((both * gains).reshape(32, 8, 256), axis=0)

        dots = lax.fori_loop(0, 16, body, jnp.zeros((8, 256), jnp.float32))
        factor = stat[0:1]
        stat[8:9] = factor * factor * factor * jnp.sum(dots, axis=0, keepdims=True) * (1.0 / 4096.0)

    def flow(start, count):
        def body(i, carry):
            j = start + i
            u = dh_t[rows(j, 128), :].astype(jnp.float32) * gain_column(j)
            x = x_t[rows(j, 128), :].astype(jnp.float32)
            d_norm = (u * stat[0:1] - x * stat[8:9]).astype(jnp.bfloat16)
            total = c_t[rows(j, 128), :].astype(jnp.float32) + d_norm.astype(jnp.float32)
            out_t[rows(j, 128), :] = total.astype(jnp.bfloat16)
            return carry

        lax.fori_loop(0, count, body, 0)

    def turn_back():
        def body(i, carry):
            nat[:, rows(i, 512)] = out_t[rows(i, 512), :].T
            return carry

        lax.fori_loop(0, 8, body, 0)

    def pass_on(i):
        part = pl.ds(i * 1024, 1024)
        return remote(out_t.at[part], x_t.at[part], (cross_send, cross_recv), (i,), torus.other())

    def pass_back(i):
        part = pl.ds(i * 1024, 1024)
        return remote(out_t.at[part], c_t.at[part], (cross_send, cross_recv), (4 + i,), torus.other())

    def gathers(sends):
        sems = (send_sem, recv_sem)

        def phase_one(c):
            first, mid, last = axes_of[c]
            return Direct(torus, first, sems, (c, 0), sends, lambda i: bufs[c].at[pos[last], pos[mid], i])

        def phase_two(c):
            first, mid, last = axes_of[c]
            return Gather(torus, mid, sems, (c, 1), sends, lambda i: bufs[c].at[pos[last], i])

        def phase_three(c, delta):
            first, mid, last = axes_of[c]
            return Gather(
                torus, last, sems, (c, 2 + delta), sends, lambda i: bufs[c].at[i, torus.at(mid, delta)])

        gain_refs = (
            lambda i: gg.at[pos["z"], pos["y"], i], lambda i: gg.at[pos["z"], i], lambda i: gg.at[i])
        gains = [
            Direct(torus, "xyz"[k], (gsend_sem, grecv_sem), (k,), sends, gain_refs[k]) for k in range(3)]
        return ([phase_one(c) for c in colours], [phase_two(c) for c in colours],
                [[phase_three(c, d) for d in range(4)] for c in colours], gains)

    def all_of(items, step):
        for item in items:
            getattr(item, step)()

    @pl.when(first_core)
    def _():
        sends = []
        one, two, three, gains = gathers(sends)
        all_of(one, "start")
        gains[0].start()
        load_inputs.wait()
        turn(nat, x_t, 0, 2)
        for c in colours:
            one[c].finish()
            two[c].start()
            three[c][OWN].start()
        gains[0].finish()
        gains[1].start()
        turn(nat, x_t, 2, 4)
        for c in colours:
            two[c].forward()
            two[c].near()
            three[c][BEFORE].start()
            three[c][AFTER].start()
        gains[1].finish()
        gains[2].start()
        turn(nat, x_t, 6, 2)
        for c in colours:
            three[c][OWN].forward()
            two[c].finish()
            three[c][FAR].start()
        gains[2].finish()
        gain_columns()
        total = prepare(0, 16)
        for c in colours:
            three[c][BEFORE].forward()
            three[c][AFTER].forward()
        total = total + prepare(16, 16)
        for c in colours:
            three[c][FAR].forward()
        pl.semaphore_signal(go_sem, inc=1, device_id=torus.other(), device_id_type=MESH)
        factors(total)
        masks()
        for c in colours:
            all_of(three[c], "near")
            all_of(three[c], "finish")
        for copy in sends:
            copy.wait_send()

    @pl.when(second_core)
    def _():
        sends = []
        one, two, three, gains = gathers(sends)
        all_of(one, "start")
        gains[0].start()
        load_upstream.wait()
        all_of(one, "finish")
        all_of(two, "start")
        gains[0].finish()
        gains[1].start()
        turn(nat, c_t, 0, 4)
        all_of(two, "forward")
        gains[1].finish()
        gains[2].start()
        turn(nat, c_t, 4, 4)
        all_of(two, "near")
        all_of(two, "finish")
        gains[2].finish()
        gain_columns()
        masks()
        pl.semaphore_wait(go_sem, 1)
        for d in range(4):
            for c in colours:
                three[c][d].start()
        for d in range(4):
            for c in colours:
                three[c][d].forward()
        total = jnp.zeros((8, 256), jnp.float32)
        for i in range(4):
            pass_on(i).wait_recv()
            total = total + prepare(8 * i, 8)
        factors(total)
        for c in colours:
            all_of(three[c], "near")
            all_of(three[c], "finish")
        for copy in sends:
            copy.wait_send()

    project()
    attention_forward()

    @pl.when(first_core)
    def _():
        for h in range(4):
            mix(2 * h)
            mix(2 * h + 1)
            pass_on(h).start()
        for i in range(4):
            pass_back(i).wait_recv()

    attention_backward()

    @pl.when(second_core)
    def _():
        through()
        for i in range(4):
            flow(8 * i, 8)
            pass_back(i).start()

    sends = []
    inboxes = ((r00, r01, r02), (r10, r11, r12), (r20, r21, r22))
    sems = (ssend_sem, srecv_sem)

    def last_phase(c, delta):
        first, mid, last = axes_of[c]
        return Scatter(
            torus, last, sems, (c, 2 + delta), sends, lambda i: sums[c].at[i, torus.at(mid, delta)],
            inboxes[2][c].at[delta])

    def mid_phase(c):
        first, mid, last = axes_of[c]
        return Scatter(torus, mid, sems, (c, 1), sends, lambda i: sums[c].at[pos[last], i], inboxes[1][c])

    def first_phase(c):
        first, mid, last = axes_of[c]
        return Direct(
            torus, first, sems, (c, 0), sends, lambda i: sums[c].at[pos[last], pos[mid], i], inboxes[0][c])

    gain_refs = (lambda i: bg.at[pos["z"], pos["y"], i], lambda i: bg.at[pos["z"], i], lambda i: bg.at[i])
    gain_trips = [
        Direct(torus, "xyz"[k], (sgsend_sem, sgrecv_sem), (k,), sends, gain_refs[k], (q0, q1, q2)[k]) for k in range(3)]
    three = [[last_phase(c, d) for d in range(4)] for c in colours]
    two = [mid_phase(c) for c in colours]
    one = [first_phase(c) for c in colours]
    order = (FAR, BEFORE, AFTER, OWN)
    for d in order:
        for c in colours:
            weight_grads(c, d)
            three[c][d].start()

    @pl.when(first_core)
    def _():
        through()
        for i in range(4):
            pass_on(i).wait_send()
        flow(0, 32)

    gcol[...] = ggcol[...].T
    for j in range(32):
        i = 2 * j
        row = jnp.broadcast_to(gcol[j:j + 1, :], (8, 128))
        bg[i // 16, i // 4 % 4, i % 4] = row
        bg[i // 16, i // 4 % 4, i % 4 + 1] = row
    gain_trips[2].start()
    for d in (FAR, BEFORE, AFTER):
        for c in colours:
            three[c][d].forward()
    turn_back()
    store = pltpu.make_async_copy(nat, out_ref, local_sem.at[7])
    store.start()
    gain_trips[2].finish()
    gain_trips[1].start()
    for c in colours:
        three[c][FAR].finish()
        two[c].start_far()
    for c in colours:
        three[c][OWN].forward()
    for c in colours:
        three[c][BEFORE].finish()
        two[c].start_before()
        three[c][AFTER].finish()
        two[c].start_after()
    gain_trips[1].finish()
    gain_trips[0].start()
    for c in colours:
        two[c].forward()
        three[c][OWN].finish()
    for c in colours:
        two[c].finish()
        one[c].start()
    gain_trips[0].finish()
    all_of(one, "finish")

    def mine(c):
        return own_place(sums, c)[...].astype(jnp.float32)

    m1 = mine(1)
    key_out[:, 0:384] = mine(0)
    key_out[:, 384:512] = m1[:, 0:128]
    value_out[:, 0:256] = m1[:, 128:384]
    value_out[:, 256:512] = mine(2)
    slab = bg[pos["z"], pos["y"], pos["x"]][0:1]
    gain_out[...] = jnp.where(odd, slab[:, 64:128], slab[:, 0:64])

    for copy in sends:
        copy.wait_send()
    store.wait()

    @pl.when(second_core)
    def _():
        for i in range(4):
            pass_back(i).wait_send()


def layers(docs, gain, key_weight, value_weight, inputs, upstream):
    vmem = pl.BlockSpec(memory_space=pltpu.VMEM)
    anywhere = pl.BlockSpec(memory_space=pl.ANY)
    bf16, f32 = jnp.bfloat16, jnp.float32
    dma = pltpu.SemaphoreType.DMA
    slabs = [pltpu.VMEM((4, 4, 4, ROWS, w), bf16) for _, _, w in COLOURS] + [pltpu.VMEM((4, 4, 4, 8, 128), f32)]
    return pl.pallas_call(
        layer_kernel,
        out_shape=[
            jax.ShapeDtypeStruct((256, 4096), bf16),
            jax.ShapeDtypeStruct((ROWS, 512), f32),
            jax.ShapeDtypeStruct((ROWS, 512), f32),
            jax.ShapeDtypeStruct((1, ROWS), f32),
        ],
        in_specs=[pl.BlockSpec(memory_space=pltpu.SMEM), vmem, anywhere, anywhere, anywhere, anywhere],
        out_specs=[anywhere, vmem, vmem, vmem],
        scratch_shapes=slabs + slabs
        + [pltpu.VMEM((4, 6, 2, ROWS, w), bf16) for _, _, w in COLOURS]
        + [pltpu.VMEM((6, 2, ROWS, w), bf16) for _, _, w in COLOURS]
        + [pltpu.VMEM((3, ROWS, w), bf16) for _, _, w in COLOURS]
        + [pltpu.VMEM((3, 4, 4, 8, 128), f32), pltpu.VMEM((3, 4, 8, 128), f32), pltpu.VMEM((3, 8, 128), f32)]
        + [
            pltpu.VMEM((256, 4096), bf16),
            pltpu.VMEM((4096, 256), bf16),
            pltpu.VMEM((4096, 256), bf16),
            pltpu.VMEM((4096, 256), bf16),
            pltpu.VMEM((256, 4096), bf16),
            pltpu.VMEM((4096, 256), bf16),
            pltpu.VMEM((4096, 256), bf16),
            pltpu.VMEM((8, 128, 1024), bf16),
            pltpu.VMEM((256, 1024), bf16),
            pltpu.VMEM((1024, 256), bf16),
            pltpu.VMEM((256, 1024), bf16),
            pltpu.VMEM((256, 1024), bf16),
            pltpu.VMEM((1024, 256), bf16),
            pltpu.VMEM((128, 128), f32),
            pltpu.VMEM((128, 128), f32),
            pltpu.VMEM((2, 128, 128), f32),
            pltpu.VMEM((16, 256), f32),
        ]
        + [
            dma((8,)),
            dma((3, 6, 6)), dma((3, 6, 6)), dma((3, 3)), dma((3, 3)),
            dma((3, 6, 6)), dma((3, 6, 6)), dma((3, 3)), dma((3, 3)),
            dma((8,)), dma((8,)),
            pltpu.SemaphoreType.REGULAR,
        ],
        compiler_params=pltpu.CompilerParams(
            collective_id=0, has_side_effects=True, vmem_limit_bytes=58 * 1024 * 1024),
        name="layers",
    )(docs, gain, key_weight, value_weight, inputs, upstream)


def shards(inputs, upstream, doc_blocks, gain, key_weight, value_weight):
    flow, key_share, value_share, gain_share = layers(
        doc_blocks, gain, key_weight[0], value_weight[0], inputs.reshape(256, 4096), upstream.reshape(256, 4096))
    return (flow.reshape(1, 2, 128, 4096), key_share[None], value_share[None], gain_share)


def solution(mesh):
    in_specs = (
        P("dp", None, None),
        P("dp", None, None),
        P("dp", None),
        P("section", "dp"),
        P("section", "dp", None),
        P("section", "dp", None),
    )
    out_specs = (
        P("section", "dp", None, None),
        P("section", "dp", None),
        P("section", "dp", None),
        P("section", "dp"),
    )
    return jax.shard_map(shards, mesh=mesh, in_specs=in_specs, out_specs=out_specs, check_vma=False)
```

time: 1260 us -> 141 us (0.11)
  blocking collectives: 525 us -> 0 us
  waiting for transfers between devices: 450 us -> 0 us
  Pallas kernels: 0 us -> 135 us
  other arithmetic: 73.7 us -> 0 us
  local copies, waits for them, and re-layouts: 67.8 us -> 5.01 us
  starting transfers between devices: 48.3 us -> 0 us
  matrix products: 45.7 us -> 0 us
  loops' own time: 23.8 us -> 0 us
  between operations: 15.6 us -> 0.67 us
    unnamed x2 -> x0, blocking collectives: 525 us -> none
    reduce_scatter x2 -> x0, waiting for transfers between devices: 385 us -> none  [the longest x1 365 us: shards(): lax.psum_scatter(totals[1], 'dp', scatter_dimension=0, tiled=True)]
    pallas_call x0 -> x1, Pallas kernels: none -> 135 us  [layers(): pl.pallas_call(layer_kernel, out_shape=[jax.ShapeDtypeStruct((256, 4096),...]
    ppermute x4 -> x0, waiting for transfers between devices: 63 us -> none  [from_behind(): return lax.ppermute(x, axis, pairs)]
    ppermute x4 -> x0, starting transfers between devices: 48.1 us -> none  [from_behind(): return lax.ppermute(x, axis, pairs)]
    dot_general x20 -> x0, matrix products: 44.8 us -> none  [the longest x8 16.8 us: attend(): jnp.einsum('bqhgd,bkhd->bhgqk', query_block, key_heads, preferred_element...]
    add x6 -> x0, other arithmetic: 31.9 us -> none  [the longest x2 30.4 us: backward_step(): totals[1] + value_part]
    another operation x6 -> x0, loops' own time: 23.8 us -> none  [the longest x1 21.8 us: shards(): lax.scan(backward_step, (empty_rows, jnp.zeros_like(inputs), start_totals...]
  transfers between devices with their start and end apart: 8 -> 0, of which waited for: 5 -> 0; matrix products, arithmetic and copies ran while one was open for 3% -> 0% of each run, Pallas kernels for 0% -> 0%
where the time goes in v1:
time: 141 us
  Pallas kernels  135 us (96%)
  local copies, waits for them, and re-layouts  5.01 us (4%)
    pallas_call x1, Pallas kernels, layers(): pl.pallas_call(layer_kernel, out_shape=[jax.ShapeDtypeStruct((256, 4096),...  135 us
    unnamed x10, local copies, waits for them, and re-layouts  5.01 us

profile of v1, /device:TPU:0, one launch (start us, length us, event | category | flops | bytes accessed | tf_op | source)
XLA Modules:
  0.0 141.2 jit_solution(17585775591166250758)
XLA Ops:
  0.6 135.5 %layers.1 = (bf16[256,4096]{1,0:T(8,128)(2,1)}, f32[64,512]{1,0:T(8,128)}, f32[64,512]{1,0:T(8,128)}, f32[1,64]{1,0:T(1,128)}) custom-call(s32[2,2]{1,0:T(2,128)} %docs_ref.1, bf16[1,64]{1,0:T(2,128)(2,1)} %gain_ref.1, bf16[64,512]{1,0:T(8,128)(2,1)} %bitcast.12, bf16[64,512]{1,0:T(8,128)(2,1)} %bitcast.13, bf16[256,4096]{1,0:T(8,128)(2,1)} %bitcast.7, ...), custom_call_target="tpu_custom_call" | custom-call | tf_op jit(solution)/shard_map/layers/pallas_call | solution.py:615
  136.1 0.0 copy-start.1
  136.1 0.0 copy-start
  136.1 0.0 copy-start.2
  136.1 3.2 %copy.14 = bf16[1,2,128,4096]{3,2,1,0:T(8,128)(2,1)} copy(bf16[1,2,128,4096]{3,2,1,0:T(8,128)(2,1)} %bitcast.9) | data formatting | bytes 4194304
  139.3 0.0 copy-done.1
  139.3 0.7 copy.15
  140.0 0.0 copy-done
  140.0 0.7 copy.16
  140.6 0.0 copy-done.2
  140.6 0.5 copy.17
Async XLA Ops:
  136.1 3.2 %copy-start.1 = (f32[64,512]{1,0:T(8,128)S(1)}, f32[64,512]{1,0:T(8,128)}, u32[]{:S(2)}) copy-start(f32[64,512]{1,0:T(8,128)} %get-tuple-element.9) | copy-start | bytes 393220
  136.1 3.9 %copy-start = (f32[64,512]{1,0:T(8,128)S(1)}, f32[64,512]{1,0:T(8,128)}, u32[]{:S(2)}) copy-start(f32[64,512]{1,0:T(8,128)} %get-tuple-element.10) | copy-start | bytes 393220
  136.1 4.5 %copy-start.2 = (f32[1,64]{1,0:T(1,128)S(1)}, f32[1,64]{1,0:T(1,128)}, u32[]{:S(2)}) copy-start(f32[1,64]{1,0:T(1,128)} %get-tuple-element.19) | copy-start | bytes 772

commit v2 on v1

--- a/solution.py
+++ b/solution.py
@@ -177,7 +177,7 @@
     docs_ref, gain_ref, key_ref, value_ref, inputs_ref, upstream_ref,
     out_ref, key_out, value_out, gain_out,
     g0, g1, g2, gg, b0, b1, b2, bg, r20, r21, r22, r10, r11, r12, r00, r01, r02, q2, q1, q0,
-    nat, x_t, out_t, m_t, m_nat, c_t, dh_t, p_t, kv, kv_t, dkv, dkv_r, dkv_t, gcol, ggcol, bias, stat,
+    nat, x_t, out_t, m_t, m_nat, c_t, dh_t, p_t, kv, kv_t, dkv, dkv_r, dkv_t, gcol, bias, stat,
     local_sem, send_sem, recv_sem, gsend_sem, grecv_sem, ssend_sem, srecv_sem, sgsend_sem, sgrecv_sem, cross_send, cross_recv,
     go_sem,
 ):
@@ -215,33 +215,30 @@
 
 
     def turn(src, dst, start, count):
-        def body(i, carry):
-            dst[rows(start + i, 512), :] = src[:, rows(start + i, 512)].T
-            return carry
-
-        lax.fori_loop(0, count, body, 0)
-
-    lane = lax.broadcasted_iota(jnp.int32, (128, 128), 1)
+        for i in range(start, start + count):
+            part = slice(512 * i, 512 * i + 512)
+            dst[part, :] = src[:, part].T
 
     def gain_columns():
-        ggcol[...] = jnp.zeros_like(ggcol)
         for j in range(32):
             i = 2 * j
-            ggcol[j:j + 1, :] = (gg[i // 16, i // 4 % 4, i % 4] + gg[i // 16, i // 4 % 4, i % 4 + 1])[0:1]
-        gcol[...] = ggcol[...].T
-
-    def gain_column(j):
-        return jnp.sum(jnp.where(lane == j, gcol[...], 0.0), axis=1, keepdims=True)
+            row = gg[i // 16, i // 4 % 4, i % 4] + gg[i // 16, i // 4 % 4, i % 4 + 1]
+            gcol[128 * j:128 * j + 128, :] = jnp.broadcast_to(row[0:1], (128, 128)).T.astype(jnp.bfloat16)
+
+    def gains_of(part):
+        once = gcol[part, :].astype(jnp.float32)
+        return jnp.concatenate([once, once], axis=1)
 
     def prepare(start, count):
-        def body(i, total):
-            x = x_t[rows(start + i, 128), :].astype(jnp.float32)
-            m = (x * gain_column(start + i)).astype(jnp.bfloat16)
-            m_t[rows(start + i, 128), :] = m
-            m_nat[:, rows(start + i, 128)] = m.T
-            return total + jnp.sum((x * x).reshape(16, 8, 256), axis=0)
-
-        return lax.fori_loop(0, count, body, jnp.zeros((8, 256), jnp.float32))
+        total = jnp.zeros((8, 256), jnp.float32)
+        for i in range(start, start + count):
+            part = slice(128 * i, 128 * i + 128)
+            x = x_t[part, :].astype(jnp.float32)
+            m = (x * gains_of(part)).astype(jnp.bfloat16)
+            m_t[part, :] = m
+            m_nat[:, part] = m.T
+            total = total + jnp.sum((x * x).reshape(16, 8, 256), axis=0)
+        return total
 
     def factors(total):
         mean = jnp.sum(total, axis=0, keepdims=True) * (1.0 / 4096.0)
@@ -252,12 +249,9 @@
 
     def project():
         for c, (_, start, w) in enumerate(COLOURS):
-            def body(z, total, c=c, w=w):
-                weight = jnp.concatenate([chunk_of(bufs, c, z, y)[...].reshape(256, w) for y in range(4)], axis=0)
-                return total + dot(m_nat[:, rows(z, 1024)], weight)
-
-            total = lax.fori_loop(0, 4, body, jnp.zeros((256, w), jnp.float32))
-            kv[:, start:start + w] = (total * factor_column()).astype(jnp.bfloat16)
+            weight = jnp.concatenate(
+                [chunk_of(bufs, c, z, y)[...].reshape(256, w) for z in range(4) for y in range(4)], axis=0)
+            kv[:, start:start + w] = (dot(m_nat[...], weight) * factor_column()).astype(jnp.bfloat16)
         kv_t[...] = kv[...].T
 
     def masks():
@@ -289,7 +283,7 @@
             probabilities(i)
             return carry
 
-        lax.fori_loop(0, 8, body, 0)
+        lax.fori_loop(0, 8, body, 0, unroll=8)
 
     def mix(i):
         h, b = i // 2, i % 2
@@ -315,7 +309,7 @@
                 dh_t[rows(h * 8 + j, 128), rows(b, 128)] = d_q[:, 128 * j:128 * j + 128].astype(jnp.bfloat16)
             return carry
 
-        lax.fori_loop(0, 8, body, 0)
+        lax.fori_loop(0, 8, body, 0, unroll=8)
         dkv_t[...] = dkv[...].T
         dkv_r[...] = (dkv[...].astype(jnp.float32) * factor_column()).astype(jnp.bfloat16)
 
@@ -323,53 +317,51 @@
         axes, start, w = COLOURS[c]
         mid = torus.at(axes[1], delta)
 
-        def body(n, carry):
+        for n in range(4):
             z, y = (n, mid) if axes[1] == "y" else (mid, n)
             part = dot(m_t[rows(z * 4 + y, 256), :], dkv_r[:, start:start + w]).astype(jnp.bfloat16)
             chunk_of(sums, c, z, y)[...] = part.reshape(4, ROWS, w)
-            return carry
-
-        lax.fori_loop(0, 4, body, 0)
 
     def through():
-        ggcol[...] = jnp.zeros_like(ggcol)
-
-        def body(i, carry):
-            z, y = i // 4, lax.rem(i, 4)
+        factor = stat[0:1]
+        dots = jnp.zeros((8, 256), jnp.float32)
+        for i in range(16):
+            z, y = i // 4, i % 4
+            part = slice(256 * i, 256 * i + 256)
             weight = jnp.concatenate(
                 [chunk_of(bufs, c, z, y)[...].reshape(256, w) for c, (_, _, w) in enumerate(COLOURS)], axis=1)
-            d_h = (dh_t[rows(i, 256), :].astype(jnp.float32) + dot(weight, dkv_t[...])).astype(jnp.bfloat16)
-            dh_t[rows(i, 256), :] = d_h
-            a = x_t[rows(i, 256), :].astype(jnp.float32)
-            both = d_h.astype(jnp.float32) * a
-            gains = jnp.concatenate([gain_column(2 * i), gain_column(2 * i + 1)], axis=0)
-            by_gain = jnp.sum(both * stat[0:1], axis=1, keepdims=True)
-            ggcol[...] = jnp.where(
-                lane == 2 * i, by_gain[0:128], jnp.where(lane == 2 * i + 1, by_gain[128:256], ggcol[...]))
-            return carry + jnp.sum((both * gains).reshape(32, 8, 256), axis=0)
-
-        dots = lax.fori_loop(0, 16, body, jnp.zeros((8, 256), jnp.float32))
-        factor = stat[0:1]
+            d_h = (dh_t[part, :].astype(jnp.float32) + dot(weight, dkv_t[...])).astype(jnp.bfloat16)
+            dh_t[part, :] = d_h
+            both = d_h.astype(jnp.float32) * x_t[part, :].astype(jnp.float32)
+            dots = dots + jnp.sum((both * gains_of(part)).reshape(32, 8, 256), axis=0)
         stat[8:9] = factor * factor * factor * jnp.sum(dots, axis=0, keepdims=True) * (1.0 / 4096.0)
 
+    def gain_grads():
+        lane = lax.broadcasted_iota(jnp.int32, (128, 128), 1)
+        total = jnp.zeros((128, 128), jnp.float32)
+        for j in range(32):
+            part = slice(128 * j, 128 * j + 128)
+            each = dh_t[part, :].astype(jnp.float32) * x_t[part, :].astype(jnp.float32) * stat[0:1]
+            total = jnp.where(lane == j, jnp.sum(each, axis=1, keepdims=True), total)
+        total = total.T
+        for j in range(32):
+            i = 2 * j
+            row = jnp.broadcast_to(total[j:j + 1, :], (8, 128))
+            bg[i // 16, i // 4 % 4, i % 4] = row
+            bg[i // 16, i // 4 % 4, i % 4 + 1] = row
+
     def flow(start, count):
-        def body(i, carry):
-            j = start + i
-            u = dh_t[rows(j, 128), :].astype(jnp.float32) * gain_column(j)
-            x = x_t[rows(j, 128), :].astype(jnp.float32)
+        for i in range(start, start + count):
+            part = slice(128 * i, 128 * i + 128)
+            u = dh_t[part, :].astype(jnp.float32) * gains_of(part)
+            x = x_t[part, :].astype(jnp.float32)
             d_norm = (u * stat[0:1] - x * stat[8:9]).astype(jnp.bfloat16)
-            total = c_t[rows(j, 128), :].astype(jnp.float32) + d_norm.astype(jnp.float32)
-            out_t[rows(j, 128), :] = total.astype(jnp.bfloat16)
-            return carry
-
-        lax.fori_loop(0, count, body, 0)
+            out_t[part, :] = (c_t[part, :].astype(jnp.float32) + d_norm.astype(jnp.float32)).astype(jnp.bfloat16)
 
     def turn_back():
-        def body(i, carry):
-            nat[:, rows(i, 512)] = out_t[rows(i, 512), :].T
-            return carry
-
-        lax.fori_loop(0, 8, body, 0)
+        for i in range(8):
+            part = slice(512 * i, 512 * i + 512)
+            nat[:, part] = out_t[part, :].T
 
     def pass_on(i):
         part = pl.ds(i * 1024, 1024)
@@ -549,12 +541,7 @@
             pass_on(i).wait_send()
         flow(0, 32)
 
-    gcol[...] = ggcol[...].T
-    for j in range(32):
-        i = 2 * j
-        row = jnp.broadcast_to(gcol[j:j + 1, :], (8, 128))
-        bg[i // 16, i // 4 % 4, i % 4] = row
-        bg[i // 16, i // 4 % 4, i % 4 + 1] = row
+    gain_grads()
     gain_trips[2].start()
     for d in (FAR, BEFORE, AFTER):
         for c in colours:
@@ -641,8 +628,7 @@
             pltpu.VMEM((256, 1024), bf16),
             pltpu.VMEM((256, 1024), bf16),
             pltpu.VMEM((1024, 256), bf16),
-            pltpu.VMEM((128, 128), f32),
-            pltpu.VMEM((128, 128), f32),
+            pltpu.VMEM((4096, 128), bf16),
             pltpu.VMEM((2, 128, 128), f32),
             pltpu.VMEM((16, 256), f32),
         ]

time: 141 us -> 118 us (0.84)
  Pallas kernels: 135 us -> 112 us
    pallas_call x1, Pallas kernels: 135 us -> 112 us  [layers(): pl.pallas_call(layer_kernel, out_shape=[jax.ShapeDtypeStruct((256, 4096),...]
where the time goes in v2:
time: 118 us
  Pallas kernels  112 us (95%)
  local copies, waits for them, and re-layouts  5.01 us (4%)
    pallas_call x1, Pallas kernels, layers(): pl.pallas_call(layer_kernel, out_shape=[jax.ShapeDtypeStruct((256, 4096),...  112 us
    unnamed x10, local copies, waits for them, and re-layouts  5.01 us

profile of v2, /device:TPU:0, one launch (start us, length us, event | category | flops | bytes accessed | tf_op | source)
XLA Modules:
  0.0 118.1 jit_solution(941480094042356966)
XLA Ops:
  0.6 112.5 %layers.1 = (bf16[256,4096]{1,0:T(8,128)(2,1)}, f32[64,512]{1,0:T(8,128)}, f32[64,512]{1,0:T(8,128)}, f32[1,64]{1,0:T(1,128)}) custom-call(s32[2,2]{1,0:T(2,128)} %docs_ref.1, bf16[1,64]{1,0:T(2,128)(2,1)} %gain_ref.1, bf16[64,512]{1,0:T(8,128)(2,1)} %bitcast.12, bf16[64,512]{1,0:T(8,128)(2,1)} %bitcast.13, bf16[256,4096]{1,0:T(8,128)(2,1)} %bitcast.7, ...), custom_call_target="tpu_custom_call" | custom-call | tf_op jit(solution)/shard_map/layers/pallas_call | solution.py:602
  113.1 0.0 copy-start.1
  113.1 0.0 copy-start
  113.1 0.0 copy-start.2
  113.1 3.2 %copy.14 = bf16[1,2,128,4096]{3,2,1,0:T(8,128)(2,1)} copy(bf16[1,2,128,4096]{3,2,1,0:T(8,128)(2,1)} %bitcast.9) | data formatting | bytes 4194304
  116.3 0.0 copy-done.1
  116.3 0.7 copy.15
  117.0 0.0 copy-done
  117.0 0.7 copy.16
  117.6 0.0 copy-done.2
  117.6 0.5 copy.17
Async XLA Ops:
  113.1 3.2 %copy-start.1 = (f32[64,512]{1,0:T(8,128)S(1)}, f32[64,512]{1,0:T(8,128)}, u32[]{:S(2)}) copy-start(f32[64,512]{1,0:T(8,128)} %get-tuple-element.9) | copy-start | bytes 393220
  113.1 3.9 %copy-start = (f32[64,512]{1,0:T(8,128)S(1)}, f32[64,512]{1,0:T(8,128)}, u32[]{:S(2)}) copy-start(f32[64,512]{1,0:T(8,128)} %get-tuple-element.10) | copy-start | bytes 393220
  113.1 4.5 %copy-start.2 = (f32[1,64]{1,0:T(1,128)S(1)}, f32[1,64]{1,0:T(1,128)}, u32[]{:S(2)}) copy-start(f32[1,64]{1,0:T(1,128)} %get-tuple-element.19) | copy-start | bytes 772

commit v3 on v2

--- a/solution.py
+++ b/solution.py
@@ -58,101 +58,102 @@
 
 
 class Ring:
-    def __init__(self, torus, axis, sems, index, sends):
-        self.torus, self.axis, self.sems, self.index, self.sends = torus, axis, sems, index, sends
-
-    def send(self, k, src, dst, delta):
-        copy = remote(src, dst, self.sems, self.index + (k,), self.torus.peer(self.axis, delta))
-        copy.start()
-        self.sends.append(copy)
+    def __init__(self, torus, axis, sems, index, ref_at, inbox=None):
+        self.torus, self.axis, self.sems, self.index, self.inbox = torus, axis, sems, index, inbox
+        self.blocks = [ref_at(torus.at(axis, d)) for d in range(4)]
+
+    def copy(self, k, src, dst, delta):
+        return remote(src, dst, self.sems, self.index + (k,), self.torus.peer(self.axis, delta))
 
     def arrived(self, k, ref):
-        remote(ref, ref, self.sems, self.index + (k,), self.torus.peer(self.axis, 1)).wait_recv()
+        self.copy(k, ref, ref, 1).wait_recv()
 
 
 class Gather(Ring):
-    def __init__(self, torus, axis, sems, index, sends, ref_at):
-        super().__init__(torus, axis, sems, index, sends)
-        self.blocks = [ref_at(torus.at(axis, d)) for d in range(4)]
+    def send(self, k, block, which, delta):
+        ref = half(self.blocks[block], which)
+        self.copy(k, ref, ref, delta).start()
 
     def start(self):
-        own = self.blocks[OWN]
-        for k, which, delta in ((0, 0, 1), (2, 1, 3), (1, 1, 1), (3, 0, 3)):
-            self.send(k, half(own, which), half(own, which), delta)
+        self.send(0, OWN, 0, 1)
+        self.send(2, OWN, 1, 3)
+        self.send(1, OWN, 1, 1)
+        self.send(3, OWN, 0, 3)
 
     def forward(self):
-        for k, block, which, delta in ((0, BEFORE, 0, 1), (2, AFTER, 1, 3)):
-            ref = half(self.blocks[block], which)
-            self.arrived(k, ref)
-            self.send(4 + k // 2, ref, ref, delta)
-
-    def near(self):
+        self.arrived(0, half(self.blocks[BEFORE], 0))
+        self.send(4, BEFORE, 0, 1)
+        self.arrived(2, half(self.blocks[AFTER], 1))
+        self.send(5, AFTER, 1, 3)
+
+    def finish(self):
         self.arrived(1, half(self.blocks[BEFORE], 1))
         self.arrived(3, half(self.blocks[AFTER], 0))
-
-    def finish(self):
         self.arrived(4, half(self.blocks[FAR], 0))
         self.arrived(5, half(self.blocks[FAR], 1))
 
+    def sent(self):
+        ref = half(self.blocks[OWN], 0)
+        for k in range(6):
+            self.copy(k, ref, ref, 1).wait_send()
+
 
 class Scatter(Ring):
-    def __init__(self, torus, axis, sems, index, sends, ref_at, inbox):
-        super().__init__(torus, axis, sems, index, sends)
-        self.blocks = [ref_at(torus.at(axis, d)) for d in range(4)]
-        self.inbox = inbox
-
-    def out(self, k, block, which, delta):
-        self.send(k, half(self.blocks[block], which), self.inbox.at[k], delta)
+    def send(self, k, block, which, delta):
+        self.copy(k, half(self.blocks[block], which), self.inbox.at[k], delta).start()
 
     def into(self, block, which, *slots):
         for k in slots:
             self.arrived(k, self.inbox.at[k])
         add_into(half(self.blocks[block], which), *[self.inbox.at[k] for k in slots])
 
-    def start_far(self):
-        self.out(0, FAR, 0, 1)
-        self.out(1, FAR, 1, 3)
-
-    def start_after(self):
-        self.out(2, AFTER, 1, 1)
-
-    def start_before(self):
-        self.out(3, BEFORE, 0, 3)
-
     def start(self):
-        self.start_far()
-        self.start_after()
-        self.start_before()
+        self.send(0, FAR, 0, 1)
+        self.send(1, FAR, 1, 3)
+        self.send(2, AFTER, 1, 1)
+        self.send(3, BEFORE, 0, 3)
 
     def forward(self):
         self.into(AFTER, 0, 0)
-        self.out(4, AFTER, 0, 1)
+        self.send(4, AFTER, 0, 1)
         self.into(BEFORE, 1, 1)
-        self.out(5, BEFORE, 1, 3)
+        self.send(5, BEFORE, 1, 3)
 
     def finish(self):
         self.into(OWN, 0, 3, 4)
         self.into(OWN, 1, 2, 5)
 
-
-class Direct:
-    def __init__(self, torus, axis, sems, index, sends, ref_at, inbox=None):
-        self.ring = Ring(torus, axis, sems, index, sends)
-        self.blocks = [ref_at(torus.at(axis, d)) for d in range(4)]
-        self.inbox = inbox
+    def sent(self):
+        for k in range(6):
+            self.copy(k, self.inbox.at[k], self.inbox.at[k], 1).wait_send()
+
+
+class Direct(Ring):
+    def send(self, delta):
+        if self.inbox is None:
+            self.copy(delta, self.blocks[OWN], self.blocks[OWN], delta).start()
+        else:
+            self.copy(delta, self.blocks[delta], self.inbox.at[delta], delta).start()
 
     def start(self):
-        for k, delta in ((0, 2), (1, 1), (2, 3)):
-            if self.inbox is None:
-                self.ring.send(k, self.blocks[OWN], self.blocks[OWN], delta)
-            else:
-                self.ring.send(k, self.blocks[delta], self.inbox.at[k], delta)
+        for delta in (FAR, AFTER, BEFORE):
+            self.send(delta)
+
+    def take(self, block):
+        self.arrived(4 - block, self.blocks[block])
 
     def finish(self):
-        for k, delta in ((0, 2), (1, 1), (2, 3)):
-            self.ring.arrived(k, self.blocks[4 - delta] if self.inbox is None else self.inbox.at[k])
-        if self.inbox is not None:
-            add_into(self.blocks[OWN], *[self.inbox.at[k] for k in range(3)])
+        if self.inbox is None:
+            for block in (AFTER, BEFORE, FAR):
+                self.take(block)
+        else:
+            for k in (1, 3, 2):
+                self.arrived(k, self.inbox.at[k])
+            add_into(self.blocks[OWN], *[self.inbox.at[k] for k in (1, 2, 3)])
+
+    def sent(self):
+        for k in (1, 2, 3):
+            self.copy(k, self.blocks[OWN], self.blocks[OWN], 1).wait_send()
 
 
 def chunk_of(bufs, c, z, y):
@@ -170,6 +171,8 @@
 
 
 def rows(i, size):
+    if isinstance(i, int):
+        return pl.ds(i * size, size)
     return pl.ds(pl.multiple_of(i * size, size), size)
 
 
@@ -247,12 +250,11 @@
     def factor_column():
         return stat[0:8].T[:, 0:1]
 
-    def project():
-        for c, (_, start, w) in enumerate(COLOURS):
-            weight = jnp.concatenate(
-                [chunk_of(bufs, c, z, y)[...].reshape(256, w) for z in range(4) for y in range(4)], axis=0)
-            kv[:, start:start + w] = (dot(m_nat[...], weight) * factor_column()).astype(jnp.bfloat16)
-        kv_t[...] = kv[...].T
+    def project(c):
+        _, start, w = COLOURS[c]
+        weight = jnp.concatenate(
+            [chunk_of(bufs, c, z, y)[...].reshape(256, w) for z in range(4) for y in range(4)], axis=0)
+        kv[:, start:start + w] = (dot(m_nat[...], weight) * factor_column()).astype(jnp.bfloat16)
 
     def masks():
         key = lax.broadcasted_iota(jnp.int32, (128, 128), 0)
@@ -271,19 +273,13 @@
     def token_row(row, b):
         return jnp.concatenate([stat[row:row + 1, rows(b, 128)]] * 8, axis=1)
 
-    def probabilities(i):
-        h, b = i // 2, lax.rem(i, 2)
-        scores = dot(kv[rows(b, 128), rows(h, 128)], heads(m_t, h, b))
-        weights = jnp.exp(scores * (token_row(0, b) * scale) + jnp.concatenate([bias[b]] * 8, axis=1))
-        share = 1.0 / jnp.sum(weights, axis=0, keepdims=True)
-        p_t[i] = (weights * share).astype(jnp.bfloat16)
-
     def attention_forward():
-        def body(i, carry):
-            probabilities(i)
-            return carry
-
-        lax.fori_loop(0, 8, body, 0, unroll=8)
+        for i in range(8):
+            h, b = i // 2, i % 2
+            scores = dot(kv[rows(b, 128), rows(h, 128)], heads(m_t, h, b))
+            weights = jnp.exp(scores * (token_row(0, b) * scale) + jnp.concatenate([bias[b]] * 8, axis=1))
+            share = 1.0 / jnp.sum(weights, axis=0, keepdims=True)
+            p_t[i] = (weights * share).astype(jnp.bfloat16)
 
     def mix(i):
         h, b = i // 2, i % 2
@@ -293,8 +289,10 @@
             out_t[at] = (x_t[at].astype(jnp.float32) + mixed[:, 128 * j:128 * j + 128]).astype(jnp.bfloat16)
 
     def attention_backward():
-        def body(i, carry):
-            h, b = i // 2, lax.rem(i, 2)
+        for i in range(8):
+            h, b = i // 2, i % 2
+            if b == 0:
+                pl.when(first_core)(pass_back(h).wait_recv)
             c = heads(c_t, h, b)
             p = p_t[i]
             d_p = dot(kv[rows(b, 128), rows(4 + h, 128)], c)
@@ -307,9 +305,6 @@
             d_q = dot(kv_t[rows(h, 128), rows(b, 128)], d_s.astype(jnp.bfloat16))
             for j in range(8):
                 dh_t[rows(h * 8 + j, 128), rows(b, 128)] = d_q[:, 128 * j:128 * j + 128].astype(jnp.bfloat16)
-            return carry
-
-        lax.fori_loop(0, 8, body, 0, unroll=8)
         dkv_t[...] = dkv[...].T
         dkv_r[...] = (dkv[...].astype(jnp.float32) * factor_column()).astype(jnp.bfloat16)
 
@@ -371,60 +366,57 @@
         part = pl.ds(i * 1024, 1024)
         return remote(out_t.at[part], c_t.at[part], (cross_send, cross_recv), (4 + i,), torus.other())
 
-    def gathers(sends):
-        sems = (send_sem, recv_sem)
-
-        def phase_one(c):
-            first, mid, last = axes_of[c]
-            return Direct(torus, first, sems, (c, 0), sends, lambda i: bufs[c].at[pos[last], pos[mid], i])
-
-        def phase_two(c):
-            first, mid, last = axes_of[c]
-            return Gather(torus, mid, sems, (c, 1), sends, lambda i: bufs[c].at[pos[last], i])
-
-        def phase_three(c, delta):
-            first, mid, last = axes_of[c]
-            return Gather(
-                torus, last, sems, (c, 2 + delta), sends, lambda i: bufs[c].at[i, torus.at(mid, delta)])
-
-        gain_refs = (
-            lambda i: gg.at[pos["z"], pos["y"], i], lambda i: gg.at[pos["z"], i], lambda i: gg.at[i])
-        gains = [
-            Direct(torus, "xyz"[k], (gsend_sem, grecv_sem), (k,), sends, gain_refs[k]) for k in range(3)]
-        return ([phase_one(c) for c in colours], [phase_two(c) for c in colours],
-                [[phase_three(c, d) for d in range(4)] for c in colours], gains)
-
-    def all_of(items, step):
+    sems, gain_sems = (send_sem, recv_sem), (gsend_sem, grecv_sem)
+
+    def phase_one(c):
+        first, mid, last = axes_of[c]
+        return Direct(torus, first, sems, (c, 0), lambda i: bufs[c].at[pos[last], pos[mid], i])
+
+    def phase_two(c):
+        first, mid, last = axes_of[c]
+        return Direct(torus, mid, sems, (c, 1), lambda i: bufs[c].at[pos[last], i])
+
+    def phase_three(c, delta):
+        first, mid, last = axes_of[c]
+        return Gather(torus, last, sems, (c, 2 + delta), lambda i: bufs[c].at[i, torus.at(mid, delta)])
+
+    def gain_places(buf):
+        return (lambda i: buf.at[pos["z"], pos["y"], i], lambda i: buf.at[pos["z"], i], lambda i: buf.at[i])
+
+    one = [phase_one(c) for c in colours]
+    two = [phase_two(c) for c in colours]
+    three = [[phase_three(c, d) for d in range(4)] for c in colours]
+    gains = [Direct(torus, "xyz"[k], gain_sems, (k,), gain_places(gg)[k]) for k in range(3)]
+
+    def each(items, step):
         for item in items:
             getattr(item, step)()
 
+    each(one, "start")
+    gains[0].start()
+
     @pl.when(first_core)
     def _():
-        sends = []
-        one, two, three, gains = gathers(sends)
-        all_of(one, "start")
-        gains[0].start()
         load_inputs.wait()
-        turn(nat, x_t, 0, 2)
+        turn(nat, x_t, 0, 8)
         for c in colours:
             one[c].finish()
             two[c].start()
             three[c][OWN].start()
         gains[0].finish()
         gains[1].start()
-        turn(nat, x_t, 2, 4)
-        for c in colours:
-            two[c].forward()
-            two[c].near()
-            three[c][BEFORE].start()
-            three[c][AFTER].start()
+        for block in (BEFORE, AFTER):
+            for c in colours:
+                two[c].take(block)
+                three[c][block].start()
         gains[1].finish()
         gains[2].start()
-        turn(nat, x_t, 6, 2)
+        for c in colours:
+            two[c].take(FAR)
+            three[c][FAR].start()
+        pl.semaphore_signal(go_sem, inc=1, device_id=torus.other(), device_id_type=MESH)
         for c in colours:
             three[c][OWN].forward()
-            two[c].finish()
-            three[c][FAR].start()
         gains[2].finish()
         gain_columns()
         total = prepare(0, 16)
@@ -434,40 +426,27 @@
         total = total + prepare(16, 16)
         for c in colours:
             three[c][FAR].forward()
-        pl.semaphore_signal(go_sem, inc=1, device_id=torus.other(), device_id_type=MESH)
         factors(total)
         masks()
-        for c in colours:
-            all_of(three[c], "near")
-            all_of(three[c], "finish")
-        for copy in sends:
-            copy.wait_send()
 
     @pl.when(second_core)
     def _():
-        sends = []
-        one, two, three, gains = gathers(sends)
-        all_of(one, "start")
-        gains[0].start()
         load_upstream.wait()
-        all_of(one, "finish")
-        all_of(two, "start")
+        each(one, "finish")
+        each(two, "start")
         gains[0].finish()
         gains[1].start()
-        turn(nat, c_t, 0, 4)
-        all_of(two, "forward")
+        turn(nat, c_t, 0, 8)
         gains[1].finish()
         gains[2].start()
-        turn(nat, c_t, 4, 4)
-        all_of(two, "near")
-        all_of(two, "finish")
+        each(two, "finish")
         gains[2].finish()
-        gain_columns()
-        masks()
         pl.semaphore_wait(go_sem, 1)
         for d in range(4):
             for c in colours:
                 three[c][d].start()
+        gain_columns()
+        masks()
         for d in range(4):
             for c in colours:
                 three[c][d].forward()
@@ -476,13 +455,11 @@
             pass_on(i).wait_recv()
             total = total + prepare(8 * i, 8)
         factors(total)
-        for c in colours:
-            all_of(three[c], "near")
-            all_of(three[c], "finish")
-        for copy in sends:
-            copy.wait_send()
-
-    project()
+
+    for c in colours:
+        each(three[c], "finish")
+        project(c)
+    kv_t[...] = kv[...].T
     attention_forward()
 
     @pl.when(first_core)
@@ -491,86 +468,89 @@
             mix(2 * h)
             mix(2 * h + 1)
             pass_on(h).start()
-        for i in range(4):
-            pass_back(i).wait_recv()
-
+
+    for trip in one + two + gains + three[0] + three[1] + three[2]:
+        trip.sent()
     attention_backward()
 
-    @pl.when(second_core)
-    def _():
-        through()
-        for i in range(4):
-            flow(8 * i, 8)
-            pass_back(i).start()
-
-    sends = []
+    out_sems, out_gain_sems = (ssend_sem, srecv_sem), (sgsend_sem, sgrecv_sem)
     inboxes = ((r00, r01, r02), (r10, r11, r12), (r20, r21, r22))
-    sems = (ssend_sem, srecv_sem)
 
     def last_phase(c, delta):
         first, mid, last = axes_of[c]
         return Scatter(
-            torus, last, sems, (c, 2 + delta), sends, lambda i: sums[c].at[i, torus.at(mid, delta)],
+            torus, last, out_sems, (c, 2 + delta), lambda i: sums[c].at[i, torus.at(mid, delta)],
             inboxes[2][c].at[delta])
 
     def mid_phase(c):
         first, mid, last = axes_of[c]
-        return Scatter(torus, mid, sems, (c, 1), sends, lambda i: sums[c].at[pos[last], i], inboxes[1][c])
+        return Direct(torus, mid, out_sems, (c, 1), lambda i: sums[c].at[pos[last], i], inboxes[1][c])
 
     def first_phase(c):
         first, mid, last = axes_of[c]
-        return Direct(
-            torus, first, sems, (c, 0), sends, lambda i: sums[c].at[pos[last], pos[mid], i], inboxes[0][c])
-
-    gain_refs = (lambda i: bg.at[pos["z"], pos["y"], i], lambda i: bg.at[pos["z"], i], lambda i: bg.at[i])
-    gain_trips = [
-        Direct(torus, "xyz"[k], (sgsend_sem, sgrecv_sem), (k,), sends, gain_refs[k], (q0, q1, q2)[k]) for k in range(3)]
-    three = [[last_phase(c, d) for d in range(4)] for c in colours]
-    two = [mid_phase(c) for c in colours]
-    one = [first_phase(c) for c in colours]
-    order = (FAR, BEFORE, AFTER, OWN)
-    for d in order:
+        return Direct(torus, first, out_sems, (c, 0), lambda i: sums[c].at[pos[last], pos[mid], i], inboxes[0][c])
+
+    home_three = [[last_phase(c, d) for d in range(4)] for c in colours]
+    home_two = [mid_phase(c) for c in colours]
+    home_one = [first_phase(c) for c in colours]
+    home_gains = [
+        Direct(torus, "xyz"[k], out_gain_sems, (k,), gain_places(bg)[k], (q0, q1, q2)[k]) for k in range(3)]
+
+    def send_group(d):
         for c in colours:
             weight_grads(c, d)
-            three[c][d].start()
+            home_three[c][d].start()
+
+    send_group(FAR)
+    send_group(BEFORE)
 
     @pl.when(first_core)
     def _():
-        through()
+        send_group(AFTER)
+        send_group(OWN)
         for i in range(4):
             pass_on(i).wait_send()
-        flow(0, 32)
-
+
+    through()
+    for i in range(4):
+        flow(8 * i, 8)
+        pl.when(second_core)(pass_back(i).start)
+
+    @pl.when(second_core)
+    def _():
+        send_group(AFTER)
+        send_group(OWN)
+
+    for c in colours:
+        home_three[c][FAR].forward()
+        home_three[c][BEFORE].forward()
     gain_grads()
-    gain_trips[2].start()
-    for d in (FAR, BEFORE, AFTER):
-        for c in colours:
-            three[c][d].forward()
+    home_gains[2].start()
     turn_back()
     store = pltpu.make_async_copy(nat, out_ref, local_sem.at[7])
     store.start()
-    gain_trips[2].finish()
-    gain_trips[1].start()
     for c in colours:
-        three[c][FAR].finish()
-        two[c].start_far()
+        home_three[c][AFTER].forward()
+        home_three[c][FAR].finish()
+        home_two[c].send(FAR)
+    home_gains[2].finish()
+    home_gains[1].start()
     for c in colours:
-        three[c][OWN].forward()
+        home_three[c][OWN].forward()
+        home_three[c][BEFORE].finish()
+        home_two[c].send(BEFORE)
+    home_gains[1].finish()
+    home_gains[0].start()
     for c in colours:
-        three[c][BEFORE].finish()
-        two[c].start_before()
-        three[c][AFTER].finish()
-        two[c].start_after()
-    gain_trips[1].finish()
-    gain_trips[0].start()
+        home_three[c][AFTER].finish()
+        home_two[c].send(AFTER)
     for c in colours:
-        two[c].forward()
-        three[c][OWN].finish()
+        home_three[c][OWN].finish()
     for c in colours:
-        two[c].finish()
-        one[c].start()
-    gain_trips[0].finish()
-    all_of(one, "finish")
+        home_two[c].finish()
+        home_one[c].start()
+    home_gains[0].finish()
+    each(home_one, "finish")
 
     def mine(c):
         return own_place(sums, c)[...].astype(jnp.float32)
@@ -583,14 +563,42 @@
     slab = bg[pos["z"], pos["y"], pos["x"]][0:1]
     gain_out[...] = jnp.where(odd, slab[:, 64:128], slab[:, 0:64])
 
-    for copy in sends:
-        copy.wait_send()
+    for trip in home_one + home_two + home_gains + home_three[0] + home_three[1] + home_three[2]:
+        trip.sent()
     store.wait()
 
     @pl.when(second_core)
     def _():
         for i in range(4):
             pass_back(i).wait_send()
+
+
+def results_kernel(*refs):
+    count = (len(refs) - 1) // 2
+    sem = refs[-1]
+    copies = []
+    for src, dst in zip(refs[:count], refs[count:2 * count]):
+        if src.shape[0] == 256:
+            copies += [(src.at[pl.ds(32 * i, 32)], dst.at[pl.ds(32 * i, 32)]) for i in range(8)]
+        else:
+            copies.append((src, dst))
+    copies = [pltpu.make_async_copy(src, dst, sem.at[i]) for i, (src, dst) in enumerate(copies)]
+    for copy in copies:
+        copy.start()
+    for copy in copies:
+        copy.wait()
+
+
+def results(arrays):
+    anywhere = pl.BlockSpec(memory_space=pl.ANY)
+    return pl.pallas_call(
+        results_kernel,
+        out_shape=[jax.ShapeDtypeStruct(a.shape, a.dtype) for a in arrays],
+        in_specs=[anywhere] * len(arrays),
+        out_specs=[anywhere] * len(arrays),
+        scratch_shapes=[pltpu.SemaphoreType.DMA((16,))],
+        name="results",
+    )(*arrays)
 
 
 def layers(docs, gain, key_weight, value_weight, inputs, upstream):
@@ -611,9 +619,9 @@
         out_specs=[anywhere, vmem, vmem, vmem],
         scratch_shapes=slabs + slabs
         + [pltpu.VMEM((4, 6, 2, ROWS, w), bf16) for _, _, w in COLOURS]
-        + [pltpu.VMEM((6, 2, ROWS, w), bf16) for _, _, w in COLOURS]
-        + [pltpu.VMEM((3, ROWS, w), bf16) for _, _, w in COLOURS]
-        + [pltpu.VMEM((3, 4, 4, 8, 128), f32), pltpu.VMEM((3, 4, 8, 128), f32), pltpu.VMEM((3, 8, 128), f32)]
+        + [pltpu.VMEM((4, 4, ROWS, w), bf16) for _, _, w in COLOURS]
+        + [pltpu.VMEM((4, ROWS, w), bf16) for _, _, w in COLOURS]
+        + [pltpu.VMEM((4, 4, 4, 8, 128), f32), pltpu.VMEM((4, 4, 8, 128), f32), pltpu.VMEM((4, 8, 128), f32)]
         + [
             pltpu.VMEM((256, 4096), bf16),
             pltpu.VMEM((4096, 256), bf16),
@@ -634,8 +642,8 @@
         ]
         + [
             dma((8,)),
-            dma((3, 6, 6)), dma((3, 6, 6)), dma((3, 3)), dma((3, 3)),
-            dma((3, 6, 6)), dma((3, 6, 6)), dma((3, 3)), dma((3, 3)),
+            dma((3, 6, 6)), dma((3, 6, 6)), dma((3, 4)), dma((3, 4)),
+            dma((3, 6, 6)), dma((3, 6, 6)), dma((3, 4)), dma((3, 4)),
             dma((8,)), dma((8,)),
             pltpu.SemaphoreType.REGULAR,
         ],
@@ -646,8 +654,8 @@
 
 
 def shards(inputs, upstream, doc_blocks, gain, key_weight, value_weight):
-    flow, key_share, value_share, gain_share = layers(
-        doc_blocks, gain, key_weight[0], value_weight[0], inputs.reshape(256, 4096), upstream.reshape(256, 4096))
+    flow, key_share, value_share, gain_share = results(layers(
+        doc_blocks, gain, key_weight[0], value_weight[0], inputs.reshape(256, 4096), upstream.reshape(256, 4096)))
     return (flow.reshape(1, 2, 128, 4096), key_share[None], value_share[None], gain_share)
 
 

time: 118 us -> 200 us (1.69)
  Pallas kernels: 112 us -> 199 us
  local copies, waits for them, and re-layouts: 5.01 us -> 0 us
    pallas_call x0 -> x1, Pallas kernels: none -> 72.7 us  [results(): pl.pallas_call(results_kernel, out_shape=[jax.ShapeDtypeStruct(a.shape, a...]
    pallas_call x1, Pallas kernels: 112 us -> 126 us  [layers(): pl.pallas_call(layer_kernel, out_shape=[jax.ShapeDtypeStruct((256, 4096),...]
    unnamed x10 -> x0, local copies, waits for them, and re-layouts: 5.01 us -> none
where the time goes in v3:
time: 200 us; the launch traced here: 199 us
  Pallas kernels  199 us (100%)
    pallas_call x1, Pallas kernels, layers(): pl.pallas_call(layer_kernel, out_shape=[jax.ShapeDtypeStruct((256, 4096),...  126 us
    pallas_call x1, Pallas kernels, results(): pl.pallas_call(results_kernel, out_shape=[jax.ShapeDtypeStruct(a.shape, a...  72.7 us

profile of v3, /device:TPU:0, one launch (start us, length us, event | category | flops | bytes accessed | tf_op | source)
XLA Modules:
  0.0 199.5 jit_solution(6982555901959496154)
XLA Ops:
  0.6 125.9 %layers.1 = (bf16[256,4096]{1,0:T(8,128)(2,1)}, f32[64,512]{1,0:T(8,128)}, f32[64,512]{1,0:T(8,128)}, f32[1,64]{1,0:T(1,128)}) custom-call(s32[2,2]{1,0:T(2,128)} %docs_ref.1, bf16[1,64]{1,0:T(2,128)(2,1)} %gain_ref.1, bf16[64,512]{1,0:T(8,128)(2,1)} %bitcast.9, bf16[64,512]{1,0:T(8,128)(2,1)} %bitcast.10, bf16[256,4096]{1,0:T(8,128)(2,1)} %bitcast.7, ...), custom_call_target="tpu_custom_call" | custom-call | tf_op jit(solution)/shard_map/layers/pallas_call | solution.py:610
  126.6 72.7 %results.1 = (bf16[256,4096]{1,0:T(8,128)(2,1)}, f32[64,512]{1,0:T(8,128)}, f32[64,512]{1,0:T(8,128)}, f32[1,64]{1,0:T(1,128)}) custom-call(bf16[256,4096]{1,0:T(8,128)(2,1)} %get-tuple-element.12.refs_0_, f32[64,512]{1,0:T(8,128)} %get-tuple-element.13.refs_1_, f32[64,512]{1,0:T(8,128)} %get-tuple-element.14.refs_2_, f32[1,64]{1,0:T(1,128)} %get-tuple-element.15.refs_3_), custom_call_target="tpu_custom_call" | custom-call | tf_op jit(solution)/shard_map/results/pallas_call | solution.py:594

commit v4 on v3

--- a/solution.py
+++ b/solution.py
@@ -86,11 +86,17 @@
         self.arrived(2, half(self.blocks[AFTER], 1))
         self.send(5, AFTER, 1, 3)
 
-    def finish(self):
+    def near(self):
         self.arrived(1, half(self.blocks[BEFORE], 1))
         self.arrived(3, half(self.blocks[AFTER], 0))
+
+    def far(self):
         self.arrived(4, half(self.blocks[FAR], 0))
         self.arrived(5, half(self.blocks[FAR], 1))
+
+    def finish(self):
+        self.near()
+        self.far()
 
     def sent(self):
         ref = half(self.blocks[OWN], 0)
@@ -107,11 +113,20 @@
             self.arrived(k, self.inbox.at[k])
         add_into(half(self.blocks[block], which), *[self.inbox.at[k] for k in slots])
 
-    def start(self):
+    def start_far(self):
         self.send(0, FAR, 0, 1)
         self.send(1, FAR, 1, 3)
+
+    def start_after(self):
         self.send(2, AFTER, 1, 1)
+
+    def start_before(self):
         self.send(3, BEFORE, 0, 3)
+
+    def start(self):
+        self.start_far()
+        self.start_after()
+        self.start_before()
 
     def forward(self):
         self.into(AFTER, 0, 0)
@@ -180,7 +195,7 @@
     docs_ref, gain_ref, key_ref, value_ref, inputs_ref, upstream_ref,
     out_ref, key_out, value_out, gain_out,
     g0, g1, g2, gg, b0, b1, b2, bg, r20, r21, r22, r10, r11, r12, r00, r01, r02, q2, q1, q0,
-    nat, x_t, out_t, m_t, m_nat, c_t, dh_t, p_t, kv, kv_t, dkv, dkv_r, dkv_t, gcol, bias, stat,
+    nat, x_t, out_t, m_t, m_nat, c_t, dh_t, p_t, kv_sum, kv, kv_t, dkv, dkv_r, dkv_t, gcol, bias, stat,
     local_sem, send_sem, recv_sem, gsend_sem, grecv_sem, ssend_sem, srecv_sem, sgsend_sem, sgrecv_sem, cross_send, cross_recv,
     go_sem,
 ):
@@ -250,11 +265,20 @@
     def factor_column():
         return stat[0:8].T[:, 0:1]
 
-    def project(c):
+    def group_places(c, delta):
+        mid = torus.at(axes_of[c][1], delta)
+        return [(n, mid) if axes_of[c][1] == "y" else (mid, n) for n in range(4)]
+
+    def project(c, places, begin):
         _, start, w = COLOURS[c]
-        weight = jnp.concatenate(
-            [chunk_of(bufs, c, z, y)[...].reshape(256, w) for z in range(4) for y in range(4)], axis=0)
-        kv[:, start:start + w] = (dot(m_nat[...], weight) * factor_column()).astype(jnp.bfloat16)
+        weight = jnp.concatenate([chunk_of(bufs, c, z, y)[...].reshape(256, w) for z, y in places], axis=0)
+        hidden = jnp.concatenate([m_nat[:, rows(z * 4 + y, 256)] for z, y in places], axis=1)
+        part = dot(hidden, weight)
+        kv_sum[:, start:start + w] = part if begin else kv_sum[:, start:start + w] + part
+
+    def projected():
+        kv[...] = (kv_sum[...] * factor_column()).astype(jnp.bfloat16)
+        kv_t[...] = kv[...].T
 
     def masks():
         key = lax.broadcasted_iota(jnp.int32, (128, 128), 0)
@@ -309,11 +333,8 @@
         dkv_r[...] = (dkv[...].astype(jnp.float32) * factor_column()).astype(jnp.bfloat16)
 
     def weight_grads(c, delta):
-        axes, start, w = COLOURS[c]
-        mid = torus.at(axes[1], delta)
-
-        for n in range(4):
-            z, y = (n, mid) if axes[1] == "y" else (mid, n)
+        _, start, w = COLOURS[c]
+        for z, y in group_places(c, delta):
             part = dot(m_t[rows(z * 4 + y, 256), :], dkv_r[:, start:start + w]).astype(jnp.bfloat16)
             chunk_of(sums, c, z, y)[...] = part.reshape(4, ROWS, w)
 
@@ -374,7 +395,7 @@
 
     def phase_two(c):
         first, mid, last = axes_of[c]
-        return Direct(torus, mid, sems, (c, 1), lambda i: bufs[c].at[pos[last], i])
+        return Gather(torus, mid, sems, (c, 1), lambda i: bufs[c].at[pos[last], i])
 
     def phase_three(c, delta):
         first, mid, last = axes_of[c]
@@ -395,28 +416,42 @@
     each(one, "start")
     gains[0].start()
 
-    @pl.when(first_core)
-    def _():
-        load_inputs.wait()
-        turn(nat, x_t, 0, 8)
+    def gather_middle(turned):
         for c in colours:
             one[c].finish()
             two[c].start()
             three[c][OWN].start()
         gains[0].finish()
         gains[1].start()
-        for block in (BEFORE, AFTER):
-            for c in colours:
-                two[c].take(block)
-                three[c][block].start()
+        turn(nat, turned, 0, 8)
+        for c in colours:
+            two[c].forward()
+
+    def gather_gains():
         gains[1].finish()
         gains[2].start()
         for c in colours:
-            two[c].take(FAR)
+            three[c][OWN].forward()
+
+    def arrive():
+        for d in (OWN, BEFORE, AFTER, FAR):
+            for c in colours:
+                three[c][d].finish()
+            for c in colours:
+                project(c, group_places(c, d), d == OWN)
+
+    @pl.when(first_core)
+    def _():
+        load_inputs.wait()
+        gather_middle(x_t)
+        for c in colours:
+            two[c].near()
+            three[c][BEFORE].start()
+            three[c][AFTER].start()
+        gather_gains()
+        for c in colours:
+            two[c].far()
             three[c][FAR].start()
-        pl.semaphore_signal(go_sem, inc=1, device_id=torus.other(), device_id_type=MESH)
-        for c in colours:
-            three[c][OWN].forward()
         gains[2].finish()
         gain_columns()
         total = prepare(0, 16)
@@ -426,28 +461,25 @@
         total = total + prepare(16, 16)
         for c in colours:
             three[c][FAR].forward()
+        pl.semaphore_signal(go_sem, inc=1, device_id=torus.other(), device_id_type=MESH)
         factors(total)
         masks()
+        arrive()
 
     @pl.when(second_core)
     def _():
         load_upstream.wait()
-        each(one, "finish")
-        each(two, "start")
-        gains[0].finish()
-        gains[1].start()
-        turn(nat, c_t, 0, 8)
-        gains[1].finish()
-        gains[2].start()
+        gather_middle(c_t)
+        gather_gains()
         each(two, "finish")
         gains[2].finish()
         pl.semaphore_wait(go_sem, 1)
-        for d in range(4):
+        for d in (BEFORE, AFTER, FAR):
             for c in colours:
                 three[c][d].start()
         gain_columns()
         masks()
-        for d in range(4):
+        for d in (BEFORE, AFTER, FAR):
             for c in colours:
                 three[c][d].forward()
         total = jnp.zeros((8, 256), jnp.float32)
@@ -455,11 +487,9 @@
             pass_on(i).wait_recv()
             total = total + prepare(8 * i, 8)
         factors(total)
-
-    for c in colours:
-        each(three[c], "finish")
-        project(c)
-    kv_t[...] = kv[...].T
+        arrive()
+
+    projected()
     attention_forward()
 
     @pl.when(first_core)
@@ -484,7 +514,7 @@
 
     def mid_phase(c):
         first, mid, last = axes_of[c]
-        return Direct(torus, mid, out_sems, (c, 1), lambda i: sums[c].at[pos[last], i], inboxes[1][c])
+        return Scatter(torus, mid, out_sems, (c, 1), lambda i: sums[c].at[pos[last], i], inboxes[1][c])
 
     def first_phase(c):
         first, mid, last = axes_of[c]
@@ -521,29 +551,28 @@
         send_group(AFTER)
         send_group(OWN)
 
-    for c in colours:
-        home_three[c][FAR].forward()
-        home_three[c][BEFORE].forward()
     gain_grads()
     home_gains[2].start()
+    for d in (FAR, BEFORE, AFTER, OWN):
+        for c in colours:
+            home_three[c][d].forward()
     turn_back()
     store = pltpu.make_async_copy(nat, out_ref, local_sem.at[7])
     store.start()
-    for c in colours:
-        home_three[c][AFTER].forward()
-        home_three[c][FAR].finish()
-        home_two[c].send(FAR)
     home_gains[2].finish()
     home_gains[1].start()
     for c in colours:
-        home_three[c][OWN].forward()
+        home_three[c][FAR].finish()
+        home_two[c].start_far()
+    for c in colours:
         home_three[c][BEFORE].finish()
-        home_two[c].send(BEFORE)
+        home_two[c].start_before()
+    for c in colours:
+        home_three[c][AFTER].finish()
+        home_two[c].start_after()
     home_gains[1].finish()
     home_gains[0].start()
-    for c in colours:
-        home_three[c][AFTER].finish()
-        home_two[c].send(AFTER)
+    each(home_two, "forward")
     for c in colours:
         home_three[c][OWN].finish()
     for c in colours:
@@ -574,29 +603,23 @@
 
 
 def results_kernel(*refs):
-    count = (len(refs) - 1) // 2
-    sem = refs[-1]
-    copies = []
-    for src, dst in zip(refs[:count], refs[count:2 * count]):
-        if src.shape[0] == 256:
-            copies += [(src.at[pl.ds(32 * i, 32)], dst.at[pl.ds(32 * i, 32)]) for i in range(8)]
-        else:
-            copies.append((src, dst))
-    copies = [pltpu.make_async_copy(src, dst, sem.at[i]) for i, (src, dst) in enumerate(copies)]
-    for copy in copies:
-        copy.start()
-    for copy in copies:
-        copy.wait()
+    count = len(refs) // 2
+    for src, dst in zip(refs[:count], refs[count:]):
+        dst[...] = src[...]
 
 
 def results(arrays):
-    anywhere = pl.BlockSpec(memory_space=pl.ANY)
+    def spec(a):
+        if a.shape[0] == 1:
+            return pl.BlockSpec(a.shape, lambda i: (0, 0))
+        return pl.BlockSpec((a.shape[0] // 2, a.shape[1]), lambda i: (i, 0))
+
     return pl.pallas_call(
         results_kernel,
+        grid=(2,),
         out_shape=[jax.ShapeDtypeStruct(a.shape, a.dtype) for a in arrays],
-        in_specs=[anywhere] * len(arrays),
-        out_specs=[anywhere] * len(arrays),
-        scratch_shapes=[pltpu.SemaphoreType.DMA((16,))],
+        in_specs=[spec(a) for a in arrays],
+        out_specs=[spec(a) for a in arrays],
         name="results",
     )(*arrays)
 
@@ -619,7 +642,7 @@
         out_specs=[anywhere, vmem, vmem, vmem],
         scratch_shapes=slabs + slabs
         + [pltpu.VMEM((4, 6, 2, ROWS, w), bf16) for _, _, w in COLOURS]
-        + [pltpu.VMEM((4, 4, ROWS, w), bf16) for _, _, w in COLOURS]
+        + [pltpu.VMEM((6, 2, ROWS, w), bf16) for _, _, w in COLOURS]
         + [pltpu.VMEM((4, ROWS, w), bf16) for _, _, w in COLOURS]
         + [pltpu.VMEM((4, 4, 4, 8, 128), f32), pltpu.VMEM((4, 4, 8, 128), f32), pltpu.VMEM((4, 8, 128), f32)]
         + [
@@ -631,6 +654,7 @@
             pltpu.VMEM((4096, 256), bf16),
             pltpu.VMEM((4096, 256), bf16),
             pltpu.VMEM((8, 128, 1024), bf16),
+            pltpu.VMEM((256, 1024), f32),
             pltpu.VMEM((256, 1024), bf16),
             pltpu.VMEM((1024, 256), bf16),
             pltpu.VMEM((256, 1024), bf16),

time: 200 us -> 115 us (0.57)
  Pallas kernels: 199 us -> 114 us
    pallas_call x1, Pallas kernels: 72.7 us -> 2.75 us  [results(): pl.pallas_call(results_kernel, grid=(2,), out_shape=[jax.ShapeDtypeStruct...]
    pallas_call x1, Pallas kernels: 126 us -> 112 us  [layers(): pl.pallas_call(layer_kernel, out_shape=[jax.ShapeDtypeStruct((256, 4096),...]
where the time goes in v4:
time: 115 us
  Pallas kernels  114 us (99%)
    pallas_call x1, Pallas kernels, layers(): pl.pallas_call(layer_kernel, out_shape=[jax.ShapeDtypeStruct((256, 4096),...  112 us
    pallas_call x1, Pallas kernels, results(): pl.pallas_call(results_kernel, grid=(2,), out_shape=[jax.ShapeDtypeStruct...  2.75 us

profile of v4, /device:TPU:0, one launch (start us, length us, event | category | flops | bytes accessed | tf_op | source)
XLA Modules:
  0.0 115.2 jit_solution(15906659805171962880)
XLA Ops:
  0.6 111.7 %layers.1 = (bf16[256,4096]{1,0:T(8,128)(2,1)}, f32[64,512]{1,0:T(8,128)}, f32[64,512]{1,0:T(8,128)}, f32[1,64]{1,0:T(1,128)}) custom-call(s32[2,2]{1,0:T(2,128)} %docs_ref.1, bf16[1,64]{1,0:T(2,128)(2,1)} %gain_ref.1, bf16[64,512]{1,0:T(8,128)(2,1)} %bitcast.9, bf16[64,512]{1,0:T(8,128)(2,1)} %bitcast.10, bf16[256,4096]{1,0:T(8,128)(2,1)} %bitcast.7, ...), custom_call_target="tpu_custom_call" | custom-call | tf_op jit(solution)/shard_map/layers/pallas_call | solution.py:633
  112.4 2.7 %results.1 = (bf16[256,4096]{1,0:T(8,128)(2,1)}, f32[64,512]{1,0:T(8,128)}, f32[64,512]{1,0:T(8,128)}, f32[1,64]{1,0:T(1,128)}) custom-call(bf16[256,4096]{1,0:T(8,128)(2,1)} %get-tuple-element.12.refs_0_, f32[64,512]{1,0:T(8,128)} %get-tuple-element.13.refs_1_, f32[64,512]{1,0:T(8,128)} %get-tuple-element.14.refs_2_, f32[1,64]{1,0:T(1,128)} %get-tuple-element.15.refs_3_), custom_call_target="tpu_custom_call" | custom-call | tf_op jit(solution)/shard_map/results/pallas_call | solution.py:617

commit v5 on v4

--- a/solution.py
+++ b/solution.py
@@ -29,13 +29,15 @@
     def other(self):
         return (1 - self.section, self.me)
 
-    def barrier(self):
+    def greet(self):
         sem = pltpu.get_barrier_semaphore()
         for axis in "xyz":
             for delta in (1, 2, 3):
                 pl.semaphore_signal(sem, inc=1, device_id=self.peer(axis, delta), device_id_type=MESH)
         pl.semaphore_signal(sem, inc=1, device_id=self.other(), device_id_type=MESH)
-        pl.semaphore_wait(sem, 10)
+
+    def all_here(self):
+        pl.semaphore_wait(pltpu.get_barrier_semaphore(), 10)
 
 
 def remote(src, dst, sems, index, device):
@@ -200,6 +202,7 @@
     go_sem,
 ):
     torus = Torus()
+    torus.greet()
     section, pos = torus.section, torus.pos
     bufs, sums = (g0, g1, g2), (b0, b1, b2)
     first_core, second_core = section == 0, section == 1
@@ -227,7 +230,7 @@
     still = jnp.zeros_like(gain_row)
     placed = jnp.where(odd, jnp.concatenate([still, gain_row], axis=1), jnp.concatenate([gain_row, still], axis=1))
     gg[pos["z"], pos["y"], pos["x"]] = jnp.broadcast_to(placed, (8, 128))
-    torus.barrier()
+    torus.all_here()
     for copy in local:
         copy.wait()
 
@@ -531,13 +534,11 @@
             weight_grads(c, d)
             home_three[c][d].start()
 
-    send_group(FAR)
-    send_group(BEFORE)
+    for d in (FAR, BEFORE, AFTER, OWN):
+        send_group(d)
 
     @pl.when(first_core)
     def _():
-        send_group(AFTER)
-        send_group(OWN)
         for i in range(4):
             pass_on(i).wait_send()
 
@@ -545,11 +546,6 @@
     for i in range(4):
         flow(8 * i, 8)
         pl.when(second_core)(pass_back(i).start)
-
-    @pl.when(second_core)
-    def _():
-        send_group(AFTER)
-        send_group(OWN)
 
     gain_grads()
     home_gains[2].start()

time: 115 us -> 113 us (0.983)
    pallas_call x1, Pallas kernels: 112 us -> 110 us  [layers(): pl.pallas_call(layer_kernel, out_shape=[jax.ShapeDtypeStruct((256, 4096),...]
where the time goes in v5:
time: 113 us
  Pallas kernels  113 us (100%)
    pallas_call x1, Pallas kernels, layers(): pl.pallas_call(layer_kernel, out_shape=[jax.ShapeDtypeStruct((256, 4096),...  110 us
    pallas_call x1, Pallas kernels, results(): pl.pallas_call(results_kernel, grid=(2,), out_shape=[jax.ShapeDtypeStruct...  2.75 us

profile of v5, /device:TPU:0, one launch (start us, length us, event | category | flops | bytes accessed | tf_op | source)
XLA Modules:
  0.0 113.3 jit_solution(18416374015852166021)
XLA Ops:
  0.6 109.8 %layers.1 = (bf16[256,4096]{1,0:T(8,128)(2,1)}, f32[64,512]{1,0:T(8,128)}, f32[64,512]{1,0:T(8,128)}, f32[1,64]{1,0:T(1,128)}) custom-call(s32[2,2]{1,0:T(2,128)} %docs_ref.1, bf16[1,64]{1,0:T(2,128)(2,1)} %gain_ref.1, bf16[64,512]{1,0:T(8,128)(2,1)} %bitcast.9, bf16[64,512]{1,0:T(8,128)(2,1)} %bitcast.10, bf16[256,4096]{1,0:T(8,128)(2,1)} %bitcast.7, ...), custom_call_target="tpu_custom_call" | custom-call | tf_op jit(solution)/shard_map/layers/pallas_call | solution.py:629
  110.5 2.7 %results.1 = (bf16[256,4096]{1,0:T(8,128)(2,1)}, f32[64,512]{1,0:T(8,128)}, f32[64,512]{1,0:T(8,128)}, f32[1,64]{1,0:T(1,128)}) custom-call(bf16[256,4096]{1,0:T(8,128)(2,1)} %get-tuple-element.12.refs_0_, f32[64,512]{1,0:T(8,128)} %get-tuple-element.13.refs_1_, f32[64,512]{1,0:T(8,128)} %get-tuple-element.14.refs_2_, f32[1,64]{1,0:T(1,128)} %get-tuple-element.15.refs_3_), custom_call_target="tpu_custom_call" | custom-call | tf_op jit(solution)/shard_map/results/pallas_call | solution.py:613
